TPU v7x, 32 devices: a whole 2x2x4 slice. The times are simulated.
32 devices in a mesh: dir: 8 (over z, x), coil: 4 (over y, core).
Axes of the slice: x: 2, y: 2, z: 4, core: 2. Of those that a mesh axis runs over, the one named last changes fastest.
Arguments:
- estimate: float32 [48, 2, 90000], P('dir', None, 'coil'), may hold values from -6 to 6
- coil_maps: float32 [16, 2, 1, 300, 300], P('coil'), may hold values from -1 to 1
- kspace: float32 [48, 16, 2, 1, 75, 300], P('dir', 'coil'), may hold values from -6 to 6
- lines: int32 [48, 75], P('dir'), may hold values from 0 to 299, as said below
- first_weight: float32 [48, 2, 96], replicated, may hold values from -0.625 to 0.625
- first_bias: float32 [96], replicated, may hold values from -3 to 3
- second_weight: float32 [96, 48, 2], replicated, may hold values from -0.625 to 0.625
Outputs:
- updated: float32 [48, 2, 90000], P('dir', None, 'coil')
Inputs may be any that keep to these rules, and one draw needn't show every extreme that they name: `lines`: the 75 entries of a row are distinct.
All inputs are finite; a program needn't handle non-finite values.
Results may differ from a plain program's by a relative error of at most 0.0003.
Values sent between devices are 32-bit elements; how exact they have to be, the bound alone decides.
No kernel may reach another device: no remote copies, remote signals or barrier semaphores. Data moves between devices by JAX's collectives and lax.ppermute only.
A program may use at most 320 MiB of HBM per device.

v0:
```python
import math

import jax
import jax.numpy as jnp
from jax import lax
from jax.sharding import PartitionSpec as P

NY = 300
NX = 300
INNER = 2
SLICES = 1


def transform_rows(index, length):
    columns = jnp.arange(length, dtype=jnp.int32)
    product = index[:, None] * columns[None, :] % length
    angle = 2.0 * math.pi / length * product.astype(jnp.float32)
    scale = 1.0 / math.sqrt(length)
    return (jnp.cos(angle) * scale, -jnp.sin(angle) * scale)


def data_gradient(image, coil_maps, kspace, chosen, cols_cos, cols_sin):
    highest = lax.Precision.HIGHEST
    lines_cos, lines_sin = transform_rows(chosen, NY)
    coil_real, coil_imag = (coil_maps[:, 0], coil_maps[:, 1])
    image_real, image_imag = (image[0][None], image[1][None])
    prod_real = coil_real * image_real - coil_imag * image_imag
    prod_imag = coil_real * image_imag + coil_imag * image_real
    rows_form = "ly,csyx->cslx"
    half_real = jnp.einsum(rows_form, lines_cos, prod_real, precision=highest) - jnp.einsum(
        rows_form, lines_sin, prod_imag, precision=highest
    )
    half_imag = jnp.einsum(rows_form, lines_cos, prod_imag, precision=highest) + jnp.einsum(
        rows_form, lines_sin, prod_real, precision=highest
    )
    cols_form = "cslx,xk->cslk"
    pred_real = jnp.einsum(cols_form, half_real, cols_cos, precision=highest) - jnp.einsum(
        cols_form, half_imag, cols_sin, precision=highest
    )
    pred_imag = jnp.einsum(cols_form, half_real, cols_sin, precision=highest) + jnp.einsum(
        cols_form, half_imag, cols_cos, precision=highest
    )
    diff_real = pred_real - kspace[:, 0]
    diff_imag = pred_imag - kspace[:, 1]
    back_real = jnp.einsum(cols_form, diff_real, cols_cos, precision=highest) + jnp.einsum(
        cols_form, diff_imag, cols_sin, precision=highest
    )
    back_imag = jnp.einsum(cols_form, diff_imag, cols_cos, precision=highest) - jnp.einsum(
        cols_form, diff_real, cols_sin, precision=highest
    )
    adjoint_form = "ly,cslx->csyx"
    spread_real = jnp.einsum(adjoint_form, lines_cos, back_real, precision=highest) + jnp.einsum(
        adjoint_form, lines_sin, back_imag, precision=highest
    )
    spread_imag = jnp.einsum(adjoint_form, lines_cos, back_imag, precision=highest) - jnp.einsum(
        adjoint_form, lines_sin, back_real, precision=highest
    )
    grad_real = jnp.sum(coil_real * spread_real + coil_imag * spread_imag, axis=0)
    grad_imag = jnp.sum(coil_real * spread_imag - coil_imag * spread_real, axis=0)
    return jnp.stack([grad_real, grad_imag])


def per_device(estimate, coil_maps, kspace, lines, first_weight, first_bias, second_weight):
    highest = lax.Precision.HIGHEST
    dir_local = estimate.shape[0]
    share = estimate.shape[2]
    voxels = SLICES * NY * NX
    cols_cos, cols_sin = transform_rows(jnp.arange(NX, dtype=jnp.int32), NX)
    whole = lax.all_gather(estimate, "coil", axis=2, tiled=True)
    position = lax.axis_index("coil")
    current = whole
    for step in range(INNER):
        image = current.reshape(dir_local, 2, SLICES, NY, NX)

        def one_direction(item):
            return data_gradient(item[0], coil_maps, item[1], item[2], cols_cos, cols_sin)

        terms = lax.map(one_direction, (image, kspace, lines))
        total = lax.psum(terms.reshape(dir_local, 2, voxels), "coil")
        current = current - 0.5 * total
    own = lax.dynamic_slice_in_dim(current, position * share, share, 2)
    groups = lax.axis_size("dir")
    padded_len = -(-share // groups) * groups
    padded = jnp.pad(own, ((0, 0), (0, 0), (0, padded_len - share)))
    gathered = lax.all_to_all(padded, "dir", split_axis=2, concat_axis=0, tiled=True)
    hidden = (
        jnp.einsum("drv,drh->hv", gathered, first_weight, precision=highest) + first_bias[:, None]
    )
    hidden = jnp.maximum(hidden, 0.0)
    noise = jnp.einsum("hv,hdr->drv", hidden, second_weight, precision=highest)
    returned = lax.all_to_all(noise, "dir", split_axis=0, concat_axis=2, tiled=True)
    return own - 0.5 * returned[:, :, :share]


def solution(mesh):
    return jax.shard_map(
        per_device,
        mesh=mesh,
        in_specs=(
            P("dir", None, "coil"),
            P("coil", None, None, None, None),
            P("dir", "coil", None, None, None, None),
            P("dir", None),
            P(),
            P(),
            P(),
        ),
        out_specs=P("dir", None, "coil"),
        check_vma=False,
    )
```

profile of v0, /device:TPU:0, one launch (start us, length us, event | category | flops | bytes accessed | tf_op | source)
XLA Modules:
  0.0 1764.1 jit_solution(16095695639535230010)
XLA Ops:
  6.5 23.4 %copy.76 = f32[6,2,22500]{0,1,2:T(2,128)} copy(f32[6,2,22500]{2,1,0:T(2,128)} %param.11) | data formatting | bytes 2160000 | tf_op args[0]
  30.0 9.0 copy.78
  39.0 9.1 copy.80
  48.1 521.3 %all-gather.2.cloned.1.call-done = f32[6,2,90000]{0,1,2:T(2,128)} async-done(((f32[6,2,22500]{0,1,2:T(2,128)}), f32[6,2,90000]{0,1,2:T(2,128)}) %all-gather.2.cloned.1.call-update) | async-done | bytes 4320016 | tf_op jit(solution)/shard_map/all_gather | solution.py:69
  569.4 94.8 %copy.79 = f32[6,2,1,300,300]{3,4,2,1,0:T(8,128)} copy(f32[6,2,1,300,300]{0,1,4,3,2:T(2,128)} %bitcast) | data formatting | bytes 8640000
  667.0 321.3 %while.28 = (s32[]{:T(128)}, f32[6,2,1,300,300]{4,3,1,0,2:T(8,128)}, f32[4,2,1,300,300]{3,4,0,2,1:T(8,128)}, f32[6,2,1,300,300]{3,4,2,1,0:T(8,128)}, s32[6,75]{1...) while((s32[]{:T(128)}, ...), condition=%wide.region_3.4_spmd.clone.clone, body=%wide.region_0.3_spmd.clone.clone.sunk | while | flops 5202089984 | bytes 57097048 | solution.py:78
  988.3 9.3 reshape.310
  997.7 98.8 %copy.82 = f32[6,2,90000]{2,1,0:T(2,128)} copy(f32[6,2,90000]{0,1,2:T(2,128)} %all-gather.2.cloned.1.call-done) | data formatting | bytes 8640000 | tf_op jit(solution)/shard_map/all_gather | solution.py:69
  1096.5 8.3 multiply_subtract_fusion
  1104.8 9.2 reshape.311
  1116.8 335.8 %while.29 = (s32[]{:T(128)}, f32[6,2,1,300,300]{4,3,1,0,2:T(8,128)}, f32[4,2,1,300,300]{3,4,0,2,1:T(8,128)}, f32[6,2,1,300,300]{4,3,1,0,2:T(8,128)}, s32[6,75]{1...) while((s32[]{:T(128)}, ...), condition=%wide.region_8.9_spmd.clone.clone, body=%wide.region_5.8_spmd.clone.clone.sunk | while | flops 5202089984 | bytes 58537048 | solution.py:78
  1124.7 5.2 fusion.578
  1179.6 5.2 fusion.578
  1234.5 5.2 fusion.578
  1289.7 5.2 fusion.578
  1452.6 9.3 reshape.312
  1462.0 87.7 %all-reduce.6.cloned.1.call-done = f32[6,2,90000]{2,1,0:T(2,128)} async-done(((f32[6,2,90000]{2,1,0:T(2,128)}), f32[6,2,90000]{2,1,0:T(2,128)}) %all-reduce.6.cloned.1.call-update) | async-done | bytes 4320016 | tf_op jit(solution)/shard_map/psum | solution.py:79
  1553.5 20.5 %copy.110 = f32[6,2,22500]{0,1,2:T(2,128)} copy(f32[6,2,22500]{2,1,0:T(2,128)S(1)} %dynamic-slice_subtract_fusion) | data formatting | bytes 2160000
  1574.0 16.2 pad_bitcast_fusion
  1590.2 37.7 %reshape.331 = f32[8,1,33756]{2,1,0:T(1,128)S(1)} reshape(f32[22504,2,6]{2,1,0:T(2,128)} %pad_bitcast_fusion) | data formatting | bytes 2160384
  1628.0 32.4 %all_to_all.36 = f32[8,1,33756]{2,1,0:T(1,128)S(1)} all-to-all(f32[8,1,33756]{2,1,0:T(1,128)S(1)} %reshape.331), channel_id=1, replica_groups=mesh['dir'=8,'coil'=4] {'dir'}, dimensions={0} | all-to-all | bytes 2160384 | tf_op jit(solution)/shard_map/all_to_all | solution.py:85
  1664.1 30.4 %reshape.332 = f32[22504,2,6]{2,1,0:T(2,128)} reshape(f32[8,33756]{1,0:T(8,128)S(1)} %reduce.16) | data formatting | bytes 2160384
  1694.5 27.0 %copy.88 = f32[6,2,8,2813]{3,1,0,2:T(2,128)S(1)} copy(f32[6,2,8,2813]{0,1,3,2:T(2,128)} %bitcast.502) | data formatting | bytes 2160384 | tf_op jit(solution)/shard_map/all_to_all | solution.py:85
  1724.6 29.6 %all_to_all.37 = f32[48,2,2813]{2,1,0:T(2,128)S(1)} all-to-all(f32[48,2,2813]{2,1,0:T(2,128)S(1)} %copy.92), channel_id=1, replica_groups=mesh['dir'=8,'coil'=4] {'dir'}, dimensions={0} | all-to-all | bytes 2160384 | tf_op jit(solution)/shard_map/all_to_all | solution.py:91
  (320 shorter events, 641.2 us)
Async XLA Ops:
  6.5 1715.0 %copy-start = (f32[48,2,96]{2,1,0:T(2,128)S(1)}, f32[48,2,96]{2,1,0:T(2,128)}, u32[]{:S(2)}) copy-start(f32[48,2,96]{2,1,0:T(2,128)} %param.15) | copy-start | bytes 110596
  6.5 562.9 %all-gather.2.cloned.1.call-start = ((), (), s32[]{:S(2)}) async-start(), calls=%async_computation.2 | async-start | bytes 115200000 | tf_op jit(solution)/shard_map/all_gather | solution.py:69
  30.0 1066.5 %all-reduce.4.cloned.1.call-start = ((), (), s32[]{:S(2)}) async-start(), calls=%async_computation.3 | async-start | bytes 8650752 | tf_op jit(solution)/shard_map/psum | solution.py:79
  667.8 6.5 copy-start.1
  720.6 6.5 copy-start.1
  773.5 6.5 copy-start.1
  826.2 6.5 copy-start.1
  878.9 6.5 copy-start.1
  931.9 6.5 copy-start.1
  997.6 552.1 %all-reduce.6.cloned.1.call-start = ((), (), s32[]{:S(2)}) async-start(), calls=%async_computation.4 | async-start | bytes 8650752 | tf_op jit(solution)/shard_map/psum | solution.py:79
  1124.6 8.1 copy-start.2
  1179.6 8.1 copy-start.2
  1234.5 8.1 copy-start.2
  1289.7 8.1 copy-start.2
  1344.7 8.1 copy-start.2
  1399.6 8.1 copy-start.2
  1694.5 27.1 %copy-start.4 = (f32[96]{0:T(128)S(1)}, f32[96]{0:T(128)}, u32[]{:S(2)}) copy-start(f32[96]{0:T(128)} %param.16) | copy-start | bytes 1156
  1721.5 1.1 copy-start.3
Sparse Core Ops, SparseCore 0:
  30.1 539.2 all-gather.1
  997.7 87.6 all-reduce.3
  1462.1 87.5 all-reduce.5
where the time goes:
time: 1780 us; the launch traced here: 1760 us
  waiting for transfers between devices  609 us (34%)
  matrix products  586 us (33%)
  local copies, waits for them, and re-layouts  461 us (26%)
  blocking collectives  62 us (3%)
  other arithmetic  17.8 us (1%)
    all_gather x1, waiting for transfers between devices, per_device(): whole = lax.all_gather(estimate, 'coil', axis=2, tiled=True)  521 us
    unnamed x14, local copies, waits for them, and re-layouts  241 us
    all_gather x1, local copies, waits for them, and re-layouts, per_device(): whole = lax.all_gather(estimate, 'coil', axis=2, tiled=True)  98.8 us
    psum x2, waiting for transfers between devices, per_device(): total = lax.psum(terms.reshape(dir_local, 2, voxels), 'coil')  87.7 us
    dot_general x12, matrix products, data_gradient(): jnp.einsum(rows_form, lines_cos, prod_real, precision=highest)  61.3 us
    dot_general x12, matrix products, data_gradient(): jnp.einsum(rows_form, lines_sin, prod_imag, precision=highest)  49.7 us
    dot_general x12, matrix products, data_gradient(): jnp.einsum(rows_form, lines_sin, prod_real, precision=highest)  39.7 us
    dot_general x12, matrix products, data_gradient(): jnp.einsum(cols_form, half_imag, cols_sin, precision=highest)  37.6 us
  transfers between devices with their start and end apart: 3, of which 2 were waited for; matrix products, arithmetic and copies ran while one was open for 7% of the time, Pallas kernels for 0%

commit v1 on v0

--- a/solution.py
+++ b/solution.py
@@ -1,14 +1,571 @@
+import functools
 import math
 
 import jax
 import jax.numpy as jnp
+import ml_dtypes
+import numpy as np
 from jax import lax
+from jax.experimental import pallas as pl
+from jax.experimental.pallas import tpu as pltpu
 from jax.sharding import PartitionSpec as P
 
 NY = 300
 NX = 300
 INNER = 2
 SLICES = 1
+BF = jnp.bfloat16
+F32 = jnp.float32
+ROWS = 304
+LANES = 384
+LPAD = 80
+HALF = 150
+VMEM_LIMIT = 58 * 2**20
+
+
+def split_host(table):
+    high = table.astype(ml_dtypes.bfloat16)
+    low = (table - high.astype(np.float64)).astype(ml_dtypes.bfloat16)
+    return high, low
+
+
+def host_tables():
+    index = np.outer(np.arange(NX), np.arange(NX)) % NX
+    angle = 2.0 * np.pi / NX * index
+    cos, sin = np.cos(angle) / np.sqrt(NX), np.sin(angle) / np.sqrt(NX)
+    back = np.zeros((2 * LANES, 2 * LANES))
+    back[:NX, :NX] = cos
+    back[LANES : LANES + NX, :NX] = -sin
+    back[:NX, LANES : LANES + NX] = sin
+    back[LANES : LANES + NX, LANES : LANES + NX] = cos
+    rows = np.zeros((2, NY, 2 * ROWS))
+    rows[0, :, :NY] = cos
+    rows[0, :, ROWS : ROWS + NY] = sin
+    rows[1, :, :NY] = -sin
+    rows[1, :, ROWS : ROWS + NY] = cos
+    return back, rows
+
+
+def split(value):
+    high = value.astype(BF)
+    return high, (value - high.astype(F32)).astype(BF)
+
+
+def dot(a, b):
+    return lax.dot_general(a, b, (((1,), (0,)), ((), ())), preferred_element_type=F32)
+
+
+def dot_nt(a, b):
+    return lax.dot_general(a, b, (((1,), (1,)), ((), ())), preferred_element_type=F32)
+
+
+def params():
+    return pltpu.CompilerParams(vmem_limit_bytes=VMEM_LIMIT)
+
+
+def cost(flops, nbytes):
+    return pl.CostEstimate(flops=int(flops), bytes_accessed=int(nbytes), transcendentals=0)
+
+
+def whole(shape):
+    return pl.BlockSpec(shape, lambda *_: (0,) * len(shape))
+
+
+def lines_kernel(lines_ref, rows_hi, rows_lo, cols_hi, cols_lo, w_ref, ah_ref):
+    length = lines_ref.shape[1]
+    pick = (lines_ref[0] == lax.broadcasted_iota(jnp.int32, (length, NY), 1)).astype(BF)
+    for part, (rows, cols) in enumerate(((rows_hi, cols_hi), (rows_lo, cols_lo))):
+        for out in range(2):
+            at = 2 * LPAD * part + LPAD * out
+            w_ref[0, at : at + LPAD, :] = dot(pick, rows[out]).astype(BF)
+            block = dot_nt(cols[out], pick).astype(BF)
+            if part == 0:
+                ah_ref[0, :, LPAD * out : LPAD * out + LPAD] = block
+                ah_ref[0, :, 2 * LPAD + LPAD * out : 3 * LPAD + LPAD * out] = block
+            else:
+                ah_ref[0, :, 4 * LPAD + LPAD * out : 5 * LPAD + LPAD * out] = block
+
+
+def line_matrices(lines, tables):
+    dirs, count = lines.shape
+    padded = jnp.pad(lines, ((0, 0), (0, LPAD - count)), constant_values=-1)[:, :, None]
+    rows_hi, rows_lo = split_host(tables)
+    cols_hi, cols_lo = split_host(tables.transpose(0, 2, 1))
+    return pl.pallas_call(
+        lines_kernel,
+        grid=(dirs,),
+        in_specs=[pl.BlockSpec((1, LPAD, 1), lambda d: (d, 0, 0))]
+        + [whole((2, NY, 2 * ROWS))] * 2
+        + [whole((2, 2 * ROWS, NY))] * 2,
+        out_specs=[
+            pl.BlockSpec((1, 4 * LPAD, 2 * ROWS), lambda d: (d, 0, 0)),
+            pl.BlockSpec((1, 2 * ROWS, 6 * LPAD), lambda d: (d, 0, 0)),
+        ],
+        out_shape=[
+            jax.ShapeDtypeStruct((dirs, 4 * LPAD, 2 * ROWS), BF),
+            jax.ShapeDtypeStruct((dirs, 2 * ROWS, 6 * LPAD), BF),
+        ],
+        compiler_params=params(),
+        cost_estimate=cost(6e9, 8e6),
+        name="line_matrices",
+    )(padded, jnp.asarray(rows_hi), jnp.asarray(rows_lo), jnp.asarray(cols_hi), jnp.asarray(cols_lo))
+
+
+def maps_kernel(pos_ref, maps_ref, out_ref):
+    planes = maps_ref.shape[0]
+    for half in range(2):
+
+        @pl.when(pos_ref[0] != half)
+        def _():
+            for k in range(planes):
+                out_ref[:, HALF * k : HALF * (k + 1)] = maps_ref[k, :, HALF * half : HALF * (half + 1)]
+
+
+def maps_half(pos, maps):
+    planes = maps.shape[0]
+    return pl.pallas_call(
+        maps_kernel,
+        grid_spec=pltpu.PrefetchScalarGridSpec(
+            num_scalar_prefetch=1,
+            grid=(1,),
+            in_specs=[whole((planes, NY, NX))],
+            out_specs=whole((NY, planes * HALF)),
+        ),
+        out_shape=jax.ShapeDtypeStruct((NY, planes * HALF), F32),
+        compiler_params=params(),
+        cost_estimate=cost(1e6, 8e6),
+        name="maps_half",
+    )(pos, maps)
+
+
+def estimate_kernel(pos_ref, est_ref, out_ref):
+    dirs, _, count = est_ref.shape
+    own = dirs // 2
+    rows = count // NX
+    for half in range(2):
+        for group in range(2):
+            place = 2 * (pos_ref[0] ^ half) + (pos_ref[1] ^ group)
+            for row in range(rows):
+                at = NX * row + HALF * half
+                out_ref[place, :, :, HALF * row : HALF * (row + 1)] = est_ref[
+                    own * group : own * (group + 1), :, at : at + HALF
+                ]
+
+
+def estimate_pieces(pos, estimate):
+    dirs, _, count = estimate.shape
+    shape = (4, dirs // 2, 2, count // 2)
+    return pl.pallas_call(
+        estimate_kernel,
+        grid_spec=pltpu.PrefetchScalarGridSpec(
+            num_scalar_prefetch=1,
+            grid=(1,),
+            in_specs=[whole(estimate.shape)],
+            out_specs=whole(shape),
+        ),
+        out_shape=jax.ShapeDtypeStruct(shape, F32),
+        compiler_params=params(),
+        cost_estimate=cost(1e6, 8e6),
+        name="estimate_pieces",
+    )(pos, estimate)
+
+
+def back_kernel(base_ref, k_ref, c_ref, f_hi, f_lo, ah_ref, o_ref, kf, xs, ss):
+    coils = c_ref.shape[0] // 2
+    count = k_ref.shape[2]
+    size = coils * LPAD
+
+    @pl.when(pl.program_id(0) == 0)
+    def _():
+        kf[...] = jnp.zeros_like(kf)
+
+    kf[:, :count, :NX] = k_ref[0]
+    for c in range(coils):
+        for r in range(2):
+            hi, lo = split(kf[2 * c + r])
+            xs[LPAD * c : LPAD * (c + 1), LANES * r : LANES * (r + 1)] = hi
+            xs[size + LPAD * c : size + LPAD * (c + 1), LANES * r : LANES * (r + 1)] = lo
+    t = dot(xs[...], f_hi[...])
+    t = t[:size] + t[size:] + dot(xs[:size], f_lo[...])
+    for c in range(coils):
+        for r in range(2):
+            hi, lo = split(t[LPAD * c : LPAD * (c + 1), LANES * r : LANES * (r + 1)])
+            lanes = slice(LANES * c, LANES * (c + 1))
+            ss[LPAD * r : LPAD * (r + 1), lanes] = hi
+            ss[LPAD * (2 + r) : LPAD * (3 + r), lanes] = lo
+            ss[LPAD * (4 + r) : LPAD * (5 + r), lanes] = hi
+    real, imag = None, None
+    for c0 in range(0, coils, 2):
+        y = dot(ah_ref[0], ss[:, LANES * c0 : LANES * (c0 + 2)])
+        for j in range(2):
+            cre, cim = c_ref[2 * (c0 + j)], c_ref[2 * (c0 + j) + 1]
+            yre = y[:NY, LANES * j : LANES * j + NX]
+            yim = y[ROWS : ROWS + NY, LANES * j : LANES * j + NX]
+            tre, tim = cre * yre + cim * yim, cre * yim - cim * yre
+            real = tre if real is None else real + tre
+            imag = tim if imag is None else imag + tim
+    o_ref[0, 0] = real
+    o_ref[0, 1] = imag
+
+
+def back_partial(base, dirs, kspace, maps, f_hi, f_lo, ah, name):
+    planes = maps.shape[0]
+    count = kspace.shape[2]
+    size = planes // 2 * LPAD
+    return pl.pallas_call(
+        back_kernel,
+        grid_spec=pltpu.PrefetchScalarGridSpec(
+            num_scalar_prefetch=1,
+            grid=(dirs,),
+            in_specs=[
+                pl.BlockSpec((1, planes, count, NX), lambda d, s: (s[0] + d, 0, 0, 0)),
+                whole((planes, NY, NX)),
+                whole((2 * LANES, 2 * LANES)),
+                whole((2 * LANES, 2 * LANES)),
+                pl.BlockSpec((1, 2 * ROWS, 6 * LPAD), lambda d, s: (s[0] + d, 0, 0)),
+            ],
+            out_specs=pl.BlockSpec((1, 2, NY, NX), lambda d, s: (d, 0, 0, 0)),
+            scratch_shapes=[
+                pltpu.VMEM((planes, LPAD, LANES), F32),
+                pltpu.VMEM((2 * size, 2 * LANES), BF),
+                pltpu.VMEM((6 * LPAD, planes // 2 * LANES), BF),
+            ],
+        ),
+        out_shape=jax.ShapeDtypeStruct((dirs, 2, NY, NX), F32),
+        compiler_params=params(),
+        cost_estimate=cost(9e9, 12e6),
+        name=name,
+    )(base, kspace, maps, f_hi, f_lo, ah)
+
+
+def halves_kernel(pos_ref, a_ref, b_ref, keep_ref, send_ref):
+    planes = 2 * a_ref.shape[0]
+    for half in range(2):
+        for k in range(planes):
+            lanes = slice(HALF * half, HALF * (half + 1))
+            total = a_ref[k // 2, k % 2, :, lanes] + b_ref[k // 2, k % 2, :, lanes]
+            place = slice(HALF * k, HALF * (k + 1))
+
+            @pl.when(pos_ref[0] == half)
+            def _():
+                keep_ref[:, place] = total
+
+            @pl.when(pos_ref[0] != half)
+            def _():
+                send_ref[:, place] = total
+
+
+def back_halves(pos, a, b):
+    shape = (NY, 2 * a.shape[0] * HALF)
+    return pl.pallas_call(
+        halves_kernel,
+        grid_spec=pltpu.PrefetchScalarGridSpec(
+            num_scalar_prefetch=1,
+            grid=(1,),
+            in_specs=[whole(a.shape)] * 2,
+            out_specs=[whole(shape)] * 2,
+        ),
+        out_shape=[jax.ShapeDtypeStruct(shape, F32)] * 2,
+        compiler_params=params(),
+        cost_estimate=cost(1e6, 10e6),
+        name="back_halves",
+    )(pos, a, b)
+
+
+def normal(pairs, zs, w_ref, ah_ref, xs, ss, acc):
+    groups = pairs.shape[0] // 4
+    acc[...] = jnp.zeros_like(acc)
+
+    def group(g, carry):
+        for j in range(2):
+            cre, cim = pairs[4 * g + 2 * j], pairs[4 * g + 2 * j + 1]
+            zre, zim = zs[0], zs[1]
+            lanes = slice(LANES * j, LANES * (j + 1))
+            hi, lo = split(cre * zre - cim * zim)
+            xs[:ROWS, lanes] = hi
+            xs[2 * ROWS : 3 * ROWS, lanes] = lo
+            hi, lo = split(cre * zim + cim * zre)
+            xs[ROWS : 2 * ROWS, lanes] = hi
+            xs[3 * ROWS :, lanes] = lo
+        size = 2 * LPAD
+        t = dot(w_ref[0], xs[: 2 * ROWS])
+        t = t[:size] + t[size:] + dot(w_ref[0, :size], xs[2 * ROWS :])
+        hi, lo = split(t)
+        ss[:size] = hi
+        ss[size : 2 * size] = lo
+        ss[2 * size :] = hi
+        y = dot(ah_ref[0], ss[...])
+        for j in range(2):
+            cre, cim = pairs[4 * g + 2 * j], pairs[4 * g + 2 * j + 1]
+            yre = y[:ROWS, LANES * j : LANES * (j + 1)]
+            yim = y[ROWS:, LANES * j : LANES * (j + 1)]
+            acc[0] += cre * yre + cim * yim
+            acc[1] += cre * yim - cim * yre
+        return carry
+
+    lax.fori_loop(0, groups, group, 0)
+
+
+def first_kernel(pos_ref, base_ref, own_ref, mate_ref, got_ref, gotm_ref, e0, e1, e2, e3, w_ref, ah_ref,
+                 u_ref, pairs, zs, zf, xs, ss, acc):
+    planes = own_ref.shape[0]
+    count = e0.shape[2]
+    rows = count // HALF
+    d = pl.program_id(0)
+
+    @pl.when(d == 0)
+    def _():
+        pairs[...] = jnp.zeros_like(pairs)
+        zs[...] = jnp.zeros_like(zs)
+        for part, (src, got) in enumerate(((own_ref, got_ref), (mate_ref, gotm_ref))):
+            for k in range(planes):
+                for half in range(2):
+
+                    @pl.when(pos_ref[0] == half)
+                    def _():
+                        pairs[planes * part + k, :NY, :HALF] = src[k, :, HALF * half : HALF * (half + 1)]
+
+                pairs[planes * part + k, :NY, HALF : 2 * HALF] = got[:, HALF * k : HALF * (k + 1)]
+
+    for k, piece in enumerate((e0, e1, e2, e3)):
+        start = rows * ((2 * pos_ref[0] + pos_ref[1]) ^ k)
+        for row in range(rows):
+            seg = piece[0, :, HALF * row : HALF * (row + 1)]
+            for r in range(2):
+                zf[r, pl.ds(start + row, 1), :] = seg[r : r + 1]
+    for r in range(2):
+        zs[r, :NY, :HALF] = zf[r, :NY, :]
+        zs[r, :NY, HALF : 2 * HALF] = zf[r, :NY, :]
+    normal(pairs, zs, w_ref, ah_ref, xs, ss, acc)
+    for r in range(2):
+        u_ref[0, r] = zs[r, :NY, :HALF] - 0.5 * (acc[r, :NY, :HALF] + acc[r, :NY, HALF : 2 * HALF])
+
+
+def pair_scratch(planes):
+    return [
+        pltpu.VMEM((2, ROWS, LANES), F32),
+        pltpu.VMEM((2, ROWS, HALF), F32),
+        pltpu.VMEM((4 * ROWS, 2 * LANES), BF),
+        pltpu.VMEM((6 * LPAD, 2 * LANES), BF),
+        pltpu.VMEM((2, ROWS, LANES), F32),
+    ]
+
+
+def line_specs():
+    return [
+        pl.BlockSpec((1, 4 * LPAD, 2 * ROWS), lambda d, p, s: (s[0] + d, 0, 0)),
+        pl.BlockSpec((1, 2 * ROWS, 6 * LPAD), lambda d, p, s: (s[0] + d, 0, 0)),
+    ]
+
+
+def first_step(pos, base, own, mate, got, gotm, pieces, w, ah):
+    planes = own.shape[0]
+    dirs, _, count = pieces[0].shape
+    piece = pl.BlockSpec((1, 2, count), lambda d, p, s: (d, 0, 0))
+    return pl.pallas_call(
+        first_kernel,
+        grid_spec=pltpu.PrefetchScalarGridSpec(
+            num_scalar_prefetch=2,
+            grid=(dirs,),
+            in_specs=[whole(own.shape)] * 2 + [whole(got.shape)] * 2 + [piece] * 4 + line_specs(),
+            out_specs=[
+                pl.BlockSpec((1, 2, NY, HALF), lambda d, p, s: (d, 0, 0, 0)),
+                whole((2 * planes, ROWS, LANES)),
+            ],
+            scratch_shapes=pair_scratch(planes),
+        ),
+        out_shape=[
+            jax.ShapeDtypeStruct((dirs, 2, NY, HALF), F32),
+            jax.ShapeDtypeStruct((2 * planes, ROWS, LANES), F32),
+        ],
+        compiler_params=params(),
+        cost_estimate=cost(18e9, 20e6),
+        name="first_step",
+    )(pos, base, own, mate, got, gotm, *pieces, w, ah)
+
+
+def second_kernel(pos_ref, base_ref, u_ref, keep_ref, got_ref, pairs, w_ref, ah_ref, z_ref, zs, zf, xs, ss, acc):
+    d = pl.program_id(0)
+
+    @pl.when(d == 0)
+    def _():
+        zs[...] = jnp.zeros_like(zs)
+
+    for k in range(keep_ref.shape[1] // (2 * HALF)):
+
+        @pl.when(d == k)
+        def _():
+            for r in range(2):
+                lanes = slice(HALF * (2 * k + r), HALF * (2 * k + r + 1))
+                zf[r, :NY, :] = 0.5 * (keep_ref[:, lanes] + got_ref[:, lanes])
+
+    for r in range(2):
+        z = u_ref[0, r] + zf[r, :NY, :]
+        zs[r, :NY, :HALF] = z
+        zs[r, :NY, HALF : 2 * HALF] = z
+    normal(pairs, zs, w_ref, ah_ref, xs, ss, acc)
+    for r in range(2):
+        total = 0.5 * (acc[r, :NY, :HALF] + acc[r, :NY, HALF : 2 * HALF])
+        z_ref[0, r] = zs[r, :NY, :HALF] + zf[r, :NY, :] - total
+
+
+def second_step(pos, base, u, keep, got, pairs, w, ah):
+    dirs = u.shape[0]
+    plane = pl.BlockSpec((1, 2, NY, HALF), lambda d, p, s: (d, 0, 0, 0))
+    return pl.pallas_call(
+        second_kernel,
+        grid_spec=pltpu.PrefetchScalarGridSpec(
+            num_scalar_prefetch=2,
+            grid=(dirs,),
+            in_specs=[plane] + [whole(keep.shape)] * 2 + [whole(pairs.shape)] + line_specs(),
+            out_specs=plane,
+            scratch_shapes=pair_scratch(pairs.shape[0] // 2),
+        ),
+        out_shape=jax.ShapeDtypeStruct(u.shape, F32),
+        compiler_params=params(),
+        cost_estimate=cost(18e9, 20e6),
+        name="second_step",
+    )(pos, base, u, keep, got, pairs, w, ah)
+
+
+def chunk_size(dirs):
+    return -(-(75 * HALF) // (dirs * 128)) * 128
+
+
+def flat_kernel(size, z_ref, o_ref, flat):
+    dirs = z_ref.shape[0]
+    rows = NY // 4
+    parts = o_ref.shape[0] // 4
+    for p in range(4):
+        for row in range(rows):
+            for d in range(dirs):
+                for r in range(2):
+                    flat[d, r : r + 1, HALF * row : HALF * (row + 1)] = z_ref[d, r, rows * p + row : rows * p + row + 1, :]
+        for q in range(parts):
+            o_ref[4 * q + p] = flat[:, :, size * q : size * (q + 1)]
+
+
+def flat_chunks(z, parts):
+    dirs = z.shape[0]
+    size = chunk_size(parts)
+    shape = (4 * parts, dirs, 2, size)
+    return pl.pallas_call(
+        functools.partial(flat_kernel, size),
+        grid=(1,),
+        in_specs=[whole(z.shape)],
+        out_specs=whole(shape),
+        out_shape=jax.ShapeDtypeStruct(shape, F32),
+        scratch_shapes=[pltpu.VMEM((dirs, 2, size * parts), F32)],
+        compiler_params=params(),
+        cost_estimate=cost(1e6, 5e6),
+        name="flat_chunks",
+    )(z)
+
+
+def denoise_kernel(x_ref, w1_ref, b1_ref, w2_ref, o_ref, xs):
+    parts = x_ref.shape[0] // 4
+    own, size = x_ref.shape[1], x_ref.shape[3]
+    for q in range(parts):
+        for y in range(2):
+            for core in range(2):
+                for d in range(own):
+                    at = 4 * own * q + 2 * own * core + 2 * d
+                    xs[at : at + 2, size * y : size * (y + 1)] = x_ref[4 * q + 2 * y + core, d]
+    w1h, w1l = split(w1_ref[...])
+    w2h, w2l = split(w2_ref[...])
+    w1 = jnp.concatenate([w1h, w1h, w1l], axis=1)
+    w2 = jnp.concatenate([w2h, w2h, w2l], axis=1)
+    x = xs[...]
+    hi, lo = split(x)
+    hidden = dot(w1, jnp.concatenate([hi, lo, hi], axis=0)) + b1_ref[...]
+    hi, lo = split(jnp.maximum(hidden, 0.0))
+    noise = dot(w2, jnp.concatenate([hi, lo, hi], axis=0))
+    xs[...] = x - 0.5 * noise
+    for q in range(parts):
+        for d in range(2 * own):
+            at = 4 * own * q + 2 * d
+            o_ref[q, d] = xs[at : at + 2, :]
+
+
+def denoise(x, w1, b1, w2):
+    parts, own, size = x.shape[0] // 4, x.shape[1], x.shape[3]
+    shape = (parts, 2 * own, 2, 2 * size)
+    return pl.pallas_call(
+        denoise_kernel,
+        grid=(1,),
+        in_specs=[whole(x.shape), whole(w1.shape), whole(b1.shape), whole(w2.shape)],
+        out_specs=whole(shape),
+        out_shape=jax.ShapeDtypeStruct(shape, F32),
+        scratch_shapes=[pltpu.VMEM((4 * own * parts, 2 * size), F32)],
+        compiler_params=params(),
+        cost_estimate=cost(1e9, 3e6),
+        name="denoise",
+    )(x, w1, b1, w2)
+
+
+def rows_kernel(x_ref, o_ref, flat):
+    parts, size = x_ref.shape[0], x_ref.shape[3] // 2
+    rows = o_ref.shape[2] // NX
+    for half in range(2):
+        for q in range(parts):
+            flat[:, :, size * q : size * (q + 1)] = x_ref[q, :, :, size * half : size * (half + 1)]
+        for row in range(rows):
+            at = NX * row + HALF * half
+            o_ref[:, :, at : at + HALF] = flat[:, :, HALF * row : HALF * (row + 1)]
+
+
+def flat_rows(x, count):
+    parts, dirs, _, size = x.shape
+    return pl.pallas_call(
+        rows_kernel,
+        grid=(1,),
+        in_specs=[whole(x.shape)],
+        out_specs=whole((dirs, 2, count)),
+        out_shape=jax.ShapeDtypeStruct((dirs, 2, count), F32),
+        scratch_shapes=[pltpu.VMEM((dirs, 2, parts * size // 2), F32)],
+        compiler_params=params(),
+        cost_estimate=cost(1e6, 3e6),
+        name="flat_rows",
+    )(x)
+
+
+def paired(estimate, coil_maps, kspace, lines, first_weight, first_bias, second_weight):
+    dirs, _, share = estimate.shape
+    own_dirs = dirs // 2
+    coils = coil_maps.shape[0]
+    parts = lax.axis_size("dir")
+    back, rows = host_tables()
+    f_hi, f_lo = (jnp.asarray(t) for t in split_host(back))
+    index = lax.axis_index("coil")
+    pos = jnp.stack([index // 2, index % 2]).astype(jnp.int32)
+    mine = (own_dirs * pos[1:2]).astype(jnp.int32)
+    other = (own_dirs * (1 - pos[1:2])).astype(jnp.int32)
+
+    def swap(value, k):
+        return lax.ppermute(value, "coil", [(p, p ^ k) for p in range(4)])
+
+    maps = coil_maps.reshape(2 * coils, NY, NX)
+    mate = swap(maps, 1)
+    got = swap(maps_half(pos, maps), 2)
+    gotm = swap(got, 1)
+    pieces = estimate_pieces(pos, estimate)
+    pieces = [pieces[k] if k == 0 else swap(pieces[k], k) for k in range(4)]
+    w, ah = line_matrices(lines, rows)
+    flat_k = kspace.reshape(dirs, 2 * coils, kspace.shape[4], NX)
+    theirs = swap(back_partial(other, own_dirs, flat_k, maps, f_hi, f_lo, ah, "back_other"), 1)
+    ours = back_partial(mine, own_dirs, flat_k, maps, f_hi, f_lo, ah, "back_own")
+    keep, send = back_halves(pos, ours, theirs)
+    got_b = swap(send, 2)
+    u, pairs = first_step(pos, mine, maps, mate, got, gotm, pieces, w, ah)
+    z = second_step(pos, mine, u, keep, got_b, pairs, w, ah)
+    chunks = flat_chunks(z, parts)
+    received = lax.all_to_all(chunks, ("dir", "coil"), split_axis=0, concat_axis=0, tiled=True)
+    channels = first_bias.shape[0]
+    w1 = first_weight.reshape(-1, channels).T
+    w2 = second_weight.reshape(channels, -1).T
+    result = denoise(received, w1, first_bias[:, None], w2)
+    returned = lax.all_to_all(result, "dir", split_axis=0, concat_axis=0, tiled=True)
+    return flat_rows(returned, share)
 
 
 def transform_rows(index, length):
@@ -92,9 +649,21 @@
     return own - 0.5 * returned[:, :, :share]
 
 
+def chosen(*arrays):
+    estimate, coil_maps, kspace = arrays[:3]
+    fits = (
+        lax.axis_size("coil") == 4
+        and estimate.shape[0] % 2 == 0
+        and estimate.shape[2] * 4 == NY * NX
+        and coil_maps.shape[0] % 2 == 0
+        and kspace.shape[4] <= LPAD
+    )
+    return paired(*arrays) if fits else per_device(*arrays)
+
+
 def solution(mesh):
     return jax.shard_map(
-        per_device,
+        chosen,
         mesh=mesh,
         in_specs=(
             P("dir", None, "coil"),

time: 1780 us -> 232 us (0.13)
  matrix products: 586 us -> 0 us
  waiting for transfers between devices: 609 us -> 25.3 us
  local copies, waits for them, and re-layouts: 461 us -> 29.8 us
  Pallas kernels: 0 us -> 130 us
  blocking collectives: 62 us -> 31.3 us
    dot_general x194 -> x0, matrix products: 586 us -> none  [the longest x12 61.3 us: data_gradient(): jnp.einsum(rows_form, lines_cos, prod_real, precision=highest)]
    all_gather x1 -> x0, waiting for transfers between devices: 521 us -> none  [per_device(): whole = lax.all_gather(estimate, 'coil', axis=2, tiled=True)]
    unnamed x14, local copies, waits for them, and re-layouts: 241 us -> 10.9 us
    pallas_call x0 -> x11, Pallas kernels: none -> 130 us  [the longest x1 36.2 us: first_step(): pl.pallas_call(first_kernel, grid_spec=pltpu.PrefetchScalarGridSpec(num_s...]
    all_gather x1 -> x0, local copies, waits for them, and re-layouts: 98.8 us -> none  [per_device(): whole = lax.all_gather(estimate, 'coil', axis=2, tiled=True)]
    psum x2 -> x0, waiting for transfers between devices: 87.7 us -> none  [per_device(): total = lax.psum(terms.reshape(dir_local, 2, voxels), 'coil')]
    all_to_all x2 -> x1, blocking collectives: 62 us -> 31.3 us  [paired(): lax.all_to_all(result, 'dir', split_axis=0, concat_axis=0, tiled=True)]
    all_to_all x4 -> x0, local copies, waits for them, and re-layouts: 29 us -> none  [the longest x2 27.5 us: per_device(): lax.all_to_all(padded, 'dir', split_axis=2, concat_axis=0, tiled=True)]
  transfers between devices with their start and end apart: 3 -> 9, of which waited for: 2 -> 1; matrix products, arithmetic and copies ran while one was open for 7% -> 11% of each run, Pallas kernels for 0% -> 36%
where the time goes in v1:
time: 232 us; the launch traced here: 231 us
  Pallas kernels  130 us (56%)
  blocking collectives  31.3 us (13%)
  local copies, waits for them, and re-layouts  29.8 us (13%)
  waiting for transfers between devices  25.3 us (11%)
  starting transfers between devices  14.1 us (6%)
    pallas_call x1, Pallas kernels, first_step(): pl.pallas_call(first_kernel, grid_spec=pltpu.PrefetchScalarGridSpec(num_s...  36.2 us
    all_to_all x1, blocking collectives, paired(): lax.all_to_all(result, 'dir', split_axis=0, concat_axis=0, tiled=True)  31.3 us
    pallas_call x1, Pallas kernels, second_step(): pl.pallas_call(second_kernel, grid_spec=pltpu.PrefetchScalarGridSpec(num_...  29.6 us
    pallas_call x2, Pallas kernels, back_partial(): pl.pallas_call(back_kernel, grid_spec=pltpu.PrefetchScalarGridSpec(num_sc...  28.3 us
    all_to_all x1, waiting for transfers between devices, paired(): lax.all_to_all(chunks, ('dir', 'coil'), split_axis=0, concat_axis=0, tile...  25.3 us
    unnamed x14, local copies, waits for them, and re-layouts  10.9 us
    pallas_call x1, Pallas kernels, line_matrices(): pl.pallas_call(lines_kernel, grid=(dirs,), in_specs=[pl.BlockSpec((1, LPA...  9.33 us
    all_to_all x1, starting transfers between devices, paired(): lax.all_to_all(chunks, ('dir', 'coil'), split_axis=0, concat_axis=0, tile...  8.48 us
  transfers between devices with their start and end apart: 9, of which 1 were waited for; matrix products, arithmetic and copies ran while one was open for 11% of the time, Pallas kernels for 36%

profile of v1, /device:TPU:0, one launch (start us, length us, event | category | flops | bytes accessed | tf_op | source)
XLA Modules:
  0.0 231.5 jit_solution(1449049544656166055)
XLA Ops:
  0.0 4.2 %copy.33 = f32[4,2,1,300,300]{4,3,2,1,0:T(8,128)} copy(f32[4,2,1,300,300]{4,2,3,1,0:T(1,128)} %param.14) | data formatting | bytes 5760000
  4.8 4.6 %maps_half.1 = f32[300,1200]{1,0:T(8,128)} custom-call(s32[2]{0:T(128)} %pad_add_fusion.pos_ref, f32[8,300,300]{2,1,0:T(8,128)} %bitcast.20), custom_call_target="tpu_custom_call" | custom-call | flops 1000000 | bytes 8000000 | tf_op jit(solution)/shard_map/maps_half/pallas_call | solution.py:126
  9.5 3.0 %collective-permute-start.1 = (f32[300,1200]{1,0:T(8,128)}, f32[300,1200]{1,0:T(8,128)S(1)}, u32[]{:S(2)}, u32[]{:S(2)}) collective-permute-start(f32[300,1200]{1,0:T(8,128)} %maps_half.1), channel_id=1, source_target_pairs={{0,2},{1,3},{2,0},{3,1},{4,6},{5,7},{6,4},{7,5},{8,10},{9,11},{10,... | collective-permute-start | bytes 4320008 | tf_op jit(solution)/shard_map/ppermute | solution.py:545
  13.3 5.7 %copy.34 = f32[6,4,2,1,75,300]{5,4,3,2,1,0:T(8,128)} copy(f32[6,4,2,1,75,300]{5,3,4,2,1,0:T(1,128)} %param.15) | data formatting | bytes 8640000
  19.0 9.3 %line_matrices.1 = (bf16[6,320,608]{2,1,0:T(8,128)(2,1)}, bf16[6,608,480]{2,1,0:T(8,128)(2,1)}) custom-call(s32[6,80,1]{2,1,0:T(8,128)} %copy.23.lines_ref, bf16[2,300,608]{2,1,0:T(8,128)(2,1)} %constant.47.clone.rows_hi, bf16[2,300,608]{2,1,0:T(8,128)(2,1)} %constant.48.clone.rows_lo, bf16[2,608,300]{2,1,0:T(8,128)(2,1)} %constant.49.clone.cols_hi, ...), custom_call_target="tpu_custom_call" | custom-call | flops 6000000000 | bytes 8000000 | tf_op jit(solution)/shard_map/line_matrices/pallas_call | solution.py:94
  28.4 14.1 %back_other.1 = f32[3,2,300,300]{3,2,1,0:T(8,128)} custom-call(s32[1]{0:T(128)S(6)} %mul.7.base_ref, f32[6,8,75,300]{3,2,1,0:T(8,128)} %bitcast.25, f32[8,300,300]{2,1,0:T(8,128)} %bitcast.21, bf16[768,768]{1,0:T(8,128)(2,1)} %constant.45.clone.f_hi, bf16[768,768]{1,0:T(8,128)(2,1)} %constant.46.clone.f_lo, bf16[6,608,480]{2,1,0:T(8,128)(2,1)} %get-tuple-element.12.ah_ref), custom_call_target="tpu_custom_call" | custom-call | flops 8999999488 | bytes 12000000 | tf_op jit(solution)/shard_map/back_other/pallas_call | solution.py:215
  42.5 5.0 %copy.28 = f32[3,2,300,300]{3,1,2,0:T(2,128)} copy(f32[3,2,300,300]{3,2,1,0:T(8,128)} %back_other.1) | data formatting | bytes 4320000 | tf_op jit(solution)/shard_map/back_other/pallas_call | solution.py:215
  47.5 3.0 %copy.22 = f32[8,300,300]{2,0,1:T(8,128)} copy(f32[8,300,300]{2,1,0:T(8,128)S(1)} %bitcast.24) | data formatting | bytes 5760000 | tf_op jit(solution)/shard_map/reshape | solution.py:547
  51.0 3.9 %estimate_pieces.1 = f32[4,3,2,11250]{3,2,1,0:T(2,128)} custom-call(s32[2]{0:T(128)} %pad_add_fusion.pos_ref, f32[6,2,22500]{2,1,0:T(2,128)} %est_ref.1), custom_call_target="tpu_custom_call" | custom-call | flops 1000000 | bytes 8000000 | tf_op jit(solution)/shard_map/estimate_pieces/pallas_call | solution.py:158
  54.9 2.5 %slice_bitcast_fusion = (f32[3,2,11250]{2,1,0:T(2,128)S(1)}, f32[3,2,11250]{2,1,0:T(2,128)S(1)}, f32[3,2,11250]{2,1,0:T(2,128)S(1)}, f32[3,2,11250]{2,1,0:T(2,128)}) fusion(f32[4,3,2,11250]{3,2,1,0:T(2,128)} %estimate_pieces.1), kind=kLoop, calls=%fused_computation | loop fusion | bytes 2160000 | tf_op jit(solution)/shard_map/squeeze | solution.py:552
  57.4 1.9 collective-permute-start.5
  59.3 14.1 %back_own.1.a_ref = f32[3,2,300,300]{3,2,1,0:T(8,128)} custom-call(s32[1]{0:T(128)S(6)} %mul.6.base_ref, f32[6,8,75,300]{3,2,1,0:T(8,128)} %bitcast.26, f32[8,300,300]{2,1,0:T(8,128)} %bitcast.22, bf16[768,768]{1,0:T(8,128)(2,1)} %constant.45.clone.f_hi, bf16[768,768]{1,0:T(8,128)(2,1)} %constant.46.clone.f_lo, bf16[6,608,480]{2,1,0:T(8,128)(2,1)} %get-tuple-element.12.ah_ref), custom_call_target="tpu_custom_call" | custom-call | flops 8999999488 | bytes 12000000 | tf_op jit(solution)/shard_map/back_own/pallas_call | solution.py:215
  73.4 3.5 %copy.29.b_ref = f32[3,2,300,300]{3,2,1,0:T(8,128)} copy(f32[3,2,300,300]{3,1,2,0:T(2,128)} %collective-permute-done.6) | data formatting | bytes 4320000 | tf_op jit(solution)/shard_map/ppermute | solution.py:545
  76.9 6.7 %back_halves.1 = (f32[300,900]{1,0:T(8,128)}, f32[300,900]{1,0:T(8,128)}) custom-call(s32[2]{0:T(128)} %pad_add_fusion.pos_ref, f32[3,2,300,300]{3,2,1,0:T(8,128)} %back_own.1.a_ref, f32[3,2,300,300]{3,2,1,0:T(8,128)} %copy.29.b_ref), custom_call_target="tpu_custom_call" | custom-call | flops 1000000 | bytes 10000000 | tf_op jit(solution)/shard_map/back_halves/pallas_call | solution.py:260
  84.0 2.6 %copy.24.mate_ref = f32[8,300,300]{2,1,0:T(8,128)} copy(f32[8,300,300]{2,0,1:T(8,128)S(1)} %collective-permute-done) | data formatting | bytes 5760000 | tf_op jit(solution)/shard_map/ppermute | solution.py:545
  86.6 36.2 %first_step.1 = (f32[3,2,300,150]{3,2,1,0:T(8,128)}, f32[16,304,384]{2,1,0:T(8,128)}) custom-call(s32[2]{0:T(128)} %pad_add_fusion.pos_ref, s32[1]{0:T(128)S(6)} %mul.6.base_ref, f32[8,300,300]{2,1,0:T(8,128)} %bitcast.23, f32[8,300,300]{2,1,0:T(8,128)} %copy.24.mate_ref, f32[300,1200]{1,0:T(8,128)} %copy-done.5, ...), custom_call_target="tpu_custom_call" | custom-call | flops 17999998976 | bytes 20000000 | tf_op jit(solution)/shard_map/first_step/pallas_call | solution.py:365
  122.8 29.6 %second_step.1.z_ref = f32[3,2,300,150]{3,2,1,0:T(8,128)} custom-call(s32[2]{0:T(128)} %pad_add_fusion.pos_ref, s32[1]{0:T(128)S(6)} %mul.6.base_ref, f32[3,2,300,150]{3,2,1,0:T(8,128)} %get-tuple-element.13.u_ref, f32[300,900]{1,0:T(8,128)} %get-tuple-element.14.keep_ref, f32[300,900]{1,0:T(8,128)} %collective-permute-done.7.got_ref, ...), custom_call_target="tpu_custom_call" | custom-call | flops 17999998976 | bytes 20000000 | tf_op jit(solution)/shard_map/second_step/pallas_call | solution.py:415
  152.4 4.7 %flat_chunks.1 = f32[32,3,2,1408]{3,2,1,0:T(2,128)} custom-call(f32[3,2,300,150]{3,2,1,0:T(8,128)} %second_step.1.z_ref), custom_call_target="tpu_custom_call" | custom-call | flops 1000000 | bytes 5000000 | tf_op jit(solution)/shard_map/flat_chunks/pallas_call | solution.py:452
  157.1 8.5 %all-to-all-start = ((f32[32,3,2,1408]{3,2,1,0:T(2,128)}), f32[32,3,2,1408]{3,2,1,0:T(2,128)S(1)}, u32[]{:S(2)}, u32[]{:S(2)}) async-start(f32[32,3,2,1408]{3,2,1,0:T(2,128)} %flat_chunks.1), calls=%async_computation | async-start | bytes 2162688 | tf_op jit(solution)/shard_map/all_to_all | solution.py:562
  167.1 25.3 %all-to-all-done.x_ref = f32[32,3,2,1408]{3,2,1,0:T(2,128)S(1)} async-done(((f32[32,3,2,1408]{3,2,1,0:T(2,128)}), f32[32,3,2,1408]{3,2,1,0:T(2,128)S(1)}, u32[]{:S(2)}, u32[]{:S(2)}) %all-to-all-start) | async-done | bytes 1081376 | tf_op jit(solution)/shard_map/all_to_all | solution.py:562
  192.3 1.0 copy-done.1
  193.3 3.6 %denoise.1 = f32[8,6,2,2816]{3,2,1,0:T(2,128)} custom-call(f32[32,3,2,1408]{3,2,1,0:T(2,128)} %copy-done.1, f32[96,96]{1,0:T(8,128)} %bitcast.28, f32[96,1]{1,0:T(8,128)} %copy.31.b1_ref, f32[96,96]{1,0:T(8,128)} %bitcast.30), custom_call_target="tpu_custom_call" | custom-call | flops 1000000000 | bytes 3000000 | tf_op jit(solution)/shard_map/denoise/pallas_call | solution.py:493
  197.0 31.3 %all_to_all.10.x_ref = f32[8,6,2,2816]{3,2,1,0:T(2,128)} all-to-all(f32[8,6,2,2816]{3,2,1,0:T(2,128)} %denoise.1), channel_id=1, replica_groups=mesh['dir'=8,'coil'=4] {'dir'}, dimensions={0} | all-to-all | bytes 2162688 | tf_op jit(solution)/shard_map/all_to_all | solution.py:567
  228.2 3.2 %flat_rows.1 = f32[6,2,22500]{2,1,0:T(2,128)} custom-call(f32[8,6,2,2816]{3,2,1,0:T(2,128)} %all_to_all.10.x_ref), custom_call_target="tpu_custom_call" | custom-call | flops 1000000 | bytes 3000000 | tf_op jit(solution)/shard_map/flat_rows/pallas_call | solution.py:519
  (30 shorter events, 3.8 us)
Async XLA Ops:
  4.8 7.6 %copy-start.3 = (s32[6,75]{1,0:T(8,128)S(1)}, s32[6,75]{1,0:T(8,128)}, u32[]{:S(2)}) copy-start(s32[6,75]{1,0:T(8,128)} %param.16) | copy-start | bytes 5404
  9.5 45.4 %collective-permute-start.1 = (f32[300,1200]{1,0:T(8,128)}, f32[300,1200]{1,0:T(8,128)S(1)}, u32[]{:S(2)}, u32[]{:S(2)}) collective-permute-start(f32[300,1200]{1,0:T(8,128)} %maps_half.1), channel_id=1, source_target_pairs={{0,2},{1,3},{2,0},{3,1},{4,6},{5,7},{6,4},{7,5},{8,10},{9,11},{10,... | collective-permute-start | bytes 4320008 | tf_op jit(solution)/shard_map/ppermute | solution.py:545
  42.5 5.0 %copy-start = (f32[4,2,1,300,300]{4,3,2,1,0:T(8,128)S(1)}, f32[4,2,1,300,300]{4,3,2,1,0:T(8,128)}, u32[]{:S(2)}) copy-start(f32[4,2,1,300,300]{4,3,2,1,0:T(8,128)} %copy.33) | copy-start | bytes 8640004
  47.5 9.9 %collective-permute-start.6 = (f32[3,2,300,300]{3,1,2,0:T(2,128)}, f32[3,2,300,300]{3,1,2,0:T(2,128)}, u32[]{:S(2)}, u32[]{:S(2)}) collective-permute-start(f32[3,2,300,300]{3,1,2,0:T(2,128)} %copy.28), channel_id=1, source_target_pairs={{0,1},{1,0},{2,3},{3,2},{4,5},{5,4},{6,7},{7,6},{8,9},{9,8},{10,11... | collective-permute-start | bytes 6480008 | tf_op jit(solution)/shard_map/ppermute | solution.py:545
  50.5 33.2 %collective-permute-start = (f32[8,300,300]{2,0,1:T(8,128)}, f32[8,300,300]{2,0,1:T(8,128)S(1)}, u32[]{:S(2)}, u32[]{:S(2)}) collective-permute-start(f32[8,300,300]{2,0,1:T(8,128)} %copy.22), channel_id=1, source_target_pairs={{0,1},{1,0},{2,3},{3,2},{4,5},{5,4},{6,7},{7,6},{8,9},{9,8},{10,11... | collective-permute-start | bytes 8640008 | tf_op jit(solution)/shard_map/ppermute | solution.py:545
  54.9 18.6 %copy-start.5 = (f32[300,1200]{1,0:T(8,128)}, f32[300,1200]{1,0:T(8,128)S(1)}, u32[]{:S(2)}) copy-start(f32[300,1200]{1,0:T(8,128)S(1)} %collective-permute-done.1.got_ref) | copy-start | bytes 4320004
  54.9 31.7 %collective-permute-start.2 = (f32[300,1200]{1,0:T(8,128)S(1)}, f32[300,1200]{1,0:T(8,128)}, u32[]{:S(2)}, u32[]{:S(2)}) collective-permute-start(f32[300,1200]{1,0:T(8,128)S(1)} %collective-permute-done.1.got_ref), channel_id=1, source_target_pairs={{0,1},{1,0},{2,3},{3,2},{4,5},{5,4},{6,7},{7,6},{8,9},{9,8},{10,11... | collective-permute-start | bytes 4320008 | tf_op jit(solution)/shard_map/ppermute | solution.py:545
  57.4 29.1 %collective-permute-start.3 = (f32[3,2,11250]{2,1,0:T(2,128)S(1)}, f32[3,2,11250]{2,1,0:T(2,128)}, u32[]{:S(2)}, u32[]{:S(2)}) collective-permute-start(f32[3,2,11250]{2,1,0:T(2,128)S(1)} %get-tuple-element.19), channel_id=1, source_target_pairs={{0,1},{1,0},{2,3},{3,2},{4,5},{5,4},{6,7},{7,6},{8,9},{9,8},{10,11... | collective-permute-start | bytes 810008 | tf_op jit(solution)/shard_map/ppermute | solution.py:545
  57.4 29.1 %collective-permute-start.4 = (f32[3,2,11250]{2,1,0:T(2,128)S(1)}, f32[3,2,11250]{2,1,0:T(2,128)}, u32[]{:S(2)}, u32[]{:S(2)}) collective-permute-start(f32[3,2,11250]{2,1,0:T(2,128)S(1)} %get-tuple-element.18), channel_id=1, source_target_pairs={{0,2},{1,3},{2,0},{3,1},{4,6},{5,7},{6,4},{7,5},{8,10},{9,11},{10,... | collective-permute-start | bytes 810008 | tf_op jit(solution)/shard_map/ppermute | solution.py:545
  57.4 29.1 %collective-permute-start.5 = (f32[3,2,11250]{2,1,0:T(2,128)S(1)}, f32[3,2,11250]{2,1,0:T(2,128)}, u32[]{:S(2)}, u32[]{:S(2)}) collective-permute-start(f32[3,2,11250]{2,1,0:T(2,128)S(1)} %get-tuple-element.17), channel_id=1, source_target_pairs={{0,3},{1,2},{2,1},{3,0},{4,7},{5,6},{6,5},{7,4},{8,11},{9,10},{10,... | collective-permute-start | bytes 810008 | tf_op jit(solution)/shard_map/ppermute | solution.py:545
  83.7 39.1 %collective-permute-start.7 = (f32[300,900]{1,0:T(8,128)}, f32[300,900]{1,0:T(8,128)}, u32[]{:S(2)}, u32[]{:S(2)}) collective-permute-start(f32[300,900]{1,0:T(8,128)} %get-tuple-element.15), channel_id=1, source_target_pairs={{0,2},{1,3},{2,0},{3,1},{4,6},{5,7},{6,4},{7,5},{8,10},{9,11},{10,... | collective-permute-start | bytes 3240008 | tf_op jit(solution)/shard_map/ppermute | solution.py:545
  152.4 13.2 %copy-start.2 = (f32[48,2,96]{2,1,0:T(2,128)S(1)}, f32[48,2,96]{2,1,0:T(2,128)}, u32[]{:S(2)}) copy-start(f32[48,2,96]{2,1,0:T(2,128)} %param.17) | copy-start | bytes 110596
  157.1 9.2 %copy-start.4 = (f32[96]{0:T(128)S(1)}, f32[96]{0:T(128)}, u32[]{:S(2)}) copy-start(f32[96]{0:T(128)} %param.18) | copy-start | bytes 1156
  157.1 35.2 %all-to-all-start = ((f32[32,3,2,1408]{3,2,1,0:T(2,128)}), f32[32,3,2,1408]{3,2,1,0:T(2,128)S(1)}, u32[]{:S(2)}, u32[]{:S(2)}) async-start(f32[32,3,2,1408]{3,2,1,0:T(2,128)} %flat_chunks.1), calls=%async_computation | async-start | bytes 2162688 | tf_op jit(solution)/shard_map/all_to_all | solution.py:562
  192.3 1.0 copy-start.1

commit v2 on v1

v2 whole, which is shorter than its diff:
```python
import functools
import math

import jax
import jax.numpy as jnp
import ml_dtypes
import numpy as np
from jax import lax
from jax.experimental import pallas as pl
from jax.experimental.pallas import tpu as pltpu
from jax.sharding import PartitionSpec as P

NY = 300
NX = 300
INNER = 2
SLICES = 1
BF = jnp.bfloat16
F32 = jnp.float32
FOLD = 160
LINK = 152
ROWS = 2 * FOLD
LANES = 384
LPAD = 80
HALF = 150
BACK = 256
GROUP = 4


def split_host(table):
    high = table.astype(ml_dtypes.bfloat16)
    low = (table - high.astype(np.float64)).astype(ml_dtypes.bfloat16)
    return high, low


def host_tables():
    index = np.outer(np.arange(NX), np.arange(NX)) % NX
    angle = 2.0 * np.pi / NX * index
    cos, sin = np.cos(angle) / np.sqrt(NX), np.sin(angle) / np.sqrt(NX)
    back = np.zeros((2 * LANES, 2 * LANES))
    back[:NX, :NX] = cos
    back[LANES : LANES + NX, :NX] = -sin
    back[:NX, LANES : LANES + NX] = sin
    back[LANES : LANES + NX, LANES : LANES + NX] = cos
    rows = np.zeros((NY, ROWS))
    rows[:, : NY // 2 + 1] = cos[:, : NY // 2 + 1]
    rows[:, FOLD : FOLD + NY // 2] = sin[:, : NY // 2]
    return back, rows


def folded(row):
    return row if row <= NY // 2 else FOLD + NY - row


def split(value):
    high = value.astype(BF)
    return high, (value - high.astype(F32)).astype(BF)


def dot(a, b):
    return lax.dot_general(a, b, (((1,), (0,)), ((), ())), preferred_element_type=F32)


def dot_high(a, b, contract=(1, 0), precision=lax.Precision.HIGH):
    dims = (((contract[0],), (contract[1],)), ((), ()))
    return lax.dot_general(a, b, dims, precision=precision, preferred_element_type=F32)


def params(mib):
    return pltpu.CompilerParams(vmem_limit_bytes=mib * 2**20)


def cost(flops, nbytes):
    return pl.CostEstimate(flops=int(flops / 1000), bytes_accessed=int(nbytes / 1000), transcendentals=0)


def result(shape):
    return pl.BlockSpec(shape, lambda *_: (0,) * len(shape))


def whole(shape):
    return pl.BlockSpec(shape, lambda *_: (0,) * len(shape), pipeline_mode=pl.Buffered(1))


def lines_kernel(lines_ref, rows_ref, cols_ref, w_ref, ah_ref):
    pick = (lines_ref[0] == lax.broadcasted_iota(jnp.int32, (LPAD, NY), 1)).astype(F32)
    w_ref[0] = dot_high(pick, rows_ref[...], precision=lax.Precision.HIGHEST)
    hi, lo = split(dot_high(cols_ref[...], pick, (1, 1), precision=lax.Precision.HIGHEST))
    ah_ref[0] = jnp.concatenate(
        [v.astype(F32) for v in (hi, hi, lo)] + [jnp.zeros((ROWS, BACK - 3 * LPAD), F32)], axis=1
    ).astype(BF)


def line_matrices(lines, table):
    dirs, count = lines.shape
    padded = jnp.pad(lines, ((0, 0), (0, LPAD - count)), constant_values=-1)[:, :, None]
    tables = [jnp.asarray(t, F32) for t in (table, table.T)]
    return pl.pallas_call(
        lines_kernel,
        grid=(dirs,),
        in_specs=[pl.BlockSpec((1, LPAD, 1), lambda d: (d, 0, 0))] + [whole(t.shape) for t in tables],
        out_specs=[
            pl.BlockSpec((1, LPAD, ROWS), lambda d: (d, 0, 0)),
            pl.BlockSpec((1, ROWS, BACK), lambda d: (d, 0, 0)),
        ],
        out_shape=[
            jax.ShapeDtypeStruct((dirs, LPAD, ROWS), F32),
            jax.ShapeDtypeStruct((dirs, ROWS, BACK), BF),
        ],
        compiler_params=params(16),
        cost_estimate=cost(1e9, 1e6),
        name="line_matrices",
    )(padded, *tables)


def maps_kernel(pos_ref, maps_ref, out_ref, send_ref):
    planes = maps_ref.shape[0]
    mirror = FOLD + NY // 2
    send_ref[...] = jnp.zeros_like(send_ref)

    @pl.loop(0, planes)
    def _(k):
        out_ref[k] = jnp.zeros_like(out_ref[k])
        for row in range(NY):
            out_ref[k, folded(row), :NX] = maps_ref[k, row, 0, :]

    for half in range(2):

        @pl.when(pos_ref[0] != half)
        def _():
            for k in range(planes):
                for part in range(2):
                    send_ref[LINK * part : LINK * (part + 1), HALF * k : HALF * (k + 1)] = out_ref[
                        k, FOLD * part : FOLD * part + LINK, HALF * half : HALF * (half + 1)
                    ]


def folded_maps(pos, maps):
    planes = maps.shape[0]
    shapes = [(planes, ROWS, LANES), (2 * LINK, planes * HALF)]
    return pl.pallas_call(
        maps_kernel,
        grid_spec=pltpu.PrefetchScalarGridSpec(
            num_scalar_prefetch=1,
            grid=(1,),
            in_specs=[whole(maps.shape)],
            out_specs=[result(s) for s in shapes],
        ),
        out_shape=[jax.ShapeDtypeStruct(s, F32) for s in shapes],
        compiler_params=params(24),
        cost_estimate=cost(1e6, 12e6),
        name="folded_maps",
    )(pos, maps)


def estimate_kernel(pos_ref, est_ref, *out_refs):
    dirs, _, count = est_ref.shape
    own = dirs // 2
    rows = count // NX
    for y in range(2):

        @pl.when(pos_ref[0] == y)
        def _():
            for k, out_ref in enumerate(out_refs):
                group = pl.ds(own * (pos_ref[1] ^ (k % 2)), own)
                for row in range(rows):
                    at = NX * row + HALF * (y ^ (k // 2))
                    out_ref[:, :, HALF * row : HALF * (row + 1)] = est_ref[group, :, at : at + HALF]


def estimate_pieces(pos, estimate):
    dirs, _, count = estimate.shape
    shape = (dirs // 2, 2, count // 2)
    return pl.pallas_call(
        estimate_kernel,
        grid_spec=pltpu.PrefetchScalarGridSpec(
            num_scalar_prefetch=1,
            grid=(1,),
            in_specs=[whole(estimate.shape)],
            out_specs=[result(shape)] * 4,
        ),
        out_shape=[jax.ShapeDtypeStruct(shape, F32)] * 4,
        compiler_params=params(16),
        cost_estimate=cost(1e6, 8e6),
        name="estimate_pieces",
    )(pos, estimate)


def adjoint(y, j, rows):
    re, im = slice(2 * LANES * j, 2 * LANES * j + LANES), slice(2 * LANES * j + LANES, 2 * LANES * (j + 1))
    mirror = pl.ds(FOLD + rows.start, rows.size)
    ure, uim, vre, vim = y[rows, re], y[rows, im], y[mirror, re], y[mirror, im]
    return ((rows, ure - vim, uim + vre), (mirror, ure + vim, uim - vre))


def back_kernel(base_ref, pos_ref, k0_ref, k1_ref, c0_ref, c1_ref, f_ref, ah_ref, keep_ref, send_ref, xs, ts, ss, ys, bs):
    coils = c0_ref.shape[0] // 2
    count = k0_ref.shape[2]
    wide = 2 * LANES
    sources = [(k, m, c) for k, m in ((k0_ref, c0_ref), (k1_ref, c1_ref)) for c in range(coils)]

    @pl.when(pl.program_id(0) == 0)
    def _():
        xs[...] = jnp.zeros_like(xs)
        ss[...] = jnp.zeros_like(ss)

    for part, k_ref in enumerate((k0_ref, k1_ref)):

        @pl.loop(0, coils)
        def _(c):
            base = pl.multiple_of(LPAD * (coils * part + c), LPAD)
            for r in range(2):
                xs[pl.ds(base, count), LANES * r : LANES * r + NX] = k_ref[0, 2 * c + r, :, 0, :]

    hi, lo = split(xs[...])
    ts[...] = dot(hi, f_ref[:wide]) + dot(lo, f_ref[:wide]) + dot(hi, f_ref[wide:])

    @pl.loop(0, LPAD // 16)
    def _(i):
        at = pl.multiple_of(16 * i, 16)
        for c in range(len(sources)):
            for lane in range(0, wide, 256):
                hi, lo = split(ts[pl.ds(LPAD * c + at, 16), lane : lane + 256])
                lanes = slice(wide * c + lane, wide * c + lane + 256)
                ss[pl.ds(at, 16), lanes] = hi
                ss[pl.ds(LPAD + at, 16), lanes] = lo
                ss[pl.ds(2 * LPAD + at, 16), lanes] = hi

    ys[...] = dot(ah_ref[0], ss[...])

    @pl.loop(0, FOLD // 8)
    def _(i):
        rows = pl.ds(pl.multiple_of(8 * i, 8), 8)
        sums = [None] * 4
        for place, (_, c_ref, c) in enumerate(sources):
            for part, (at, yre, yim) in enumerate(adjoint(ys, place, rows)):
                cre, cim = c_ref[2 * c, at], c_ref[2 * c + 1, at]
                for r, term in enumerate((cre * yre + cim * yim, cre * yim - cim * yre)):
                    old = sums[2 * part + r]
                    sums[2 * part + r] = term if old is None else old + term
        for part in range(2):
            for r in range(2):
                bs[r, pl.ds(pl.multiple_of(FOLD * part + 8 * i, 8), 8), :] = sums[2 * part + r]

    for half in range(2):
        lanes = slice(HALF * half, HALF * (half + 1))

        @pl.when(pos_ref[0] == half)
        def _():
            for r in range(2):
                keep_ref[0, r] = bs[r, :, lanes]

        for k in range(send_ref.shape[1] // (2 * HALF)):

            @pl.when((pos_ref[0] != half) & (pl.program_id(0) == k))
            def _():
                for r in range(2):
                    place = slice(HALF * (2 * k + r), HALF * (2 * k + r + 1))
                    for part in range(2):
                        send_ref[LINK * part : LINK * (part + 1), place] = bs[
                            r, FOLD * part : FOLD * part + LINK, lanes
                        ]


def back_sums(base, pos, dirs, k_own, k_mate, own, mate, f_back, ah):
    _, planes, count, _, _ = k_own.shape
    link = (2 * LINK, 2 * dirs * HALF)
    k_spec = pl.BlockSpec((1, planes, count, 1, NX), lambda d, s, *_: (s[0] + d, 0, 0, 0, 0))
    return pl.pallas_call(
        back_kernel,
        grid_spec=pltpu.PrefetchScalarGridSpec(
            num_scalar_prefetch=2,
            grid=(dirs,),
            in_specs=[k_spec] * 2
            + [whole((planes, ROWS, LANES))] * 2
            + [whole(f_back.shape), pl.BlockSpec((1, ROWS, BACK), lambda d, s, *_: (s[0] + d, 0, 0))],
            out_specs=[pl.BlockSpec((1, 2, ROWS, HALF), lambda d, *_: (d, 0, 0, 0)), result(link)],
            scratch_shapes=[
                pltpu.VMEM((planes * LPAD, 2 * LANES), F32),
                pltpu.VMEM((planes * LPAD, 2 * LANES), F32),
                pltpu.VMEM((BACK, 2 * planes * LANES), BF),
                pltpu.VMEM((ROWS, 2 * planes * LANES), F32),
                pltpu.VMEM((2, ROWS, LANES), F32),
            ],
        ),
        out_shape=[jax.ShapeDtypeStruct((dirs, 2, ROWS, HALF), F32), jax.ShapeDtypeStruct(link, F32)],
        compiler_params=params(48),
        cost_estimate=cost(14e9, 22e6),
        name="back_sums",
    )(base, pos, k_own, k_mate, own, mate, f_back, ah)


def normal(pairs, zs, w_ref, ah_ref, xs, ts, ss, ys, acc):
    groups = pairs.shape[0] // (2 * GROUP)
    wide = 2 * LANES

    @pl.loop(0, groups)
    def _(g):
        @pl.loop(0, FOLD // 16)
        def _(i):
            at = pl.multiple_of(16 * i, 16)
            rows = (pl.ds(at, 16), pl.ds(FOLD + at, 16))
            for lane in range(0, LANES, 128):
                lanes = slice(lane, lane + 128)
                z = [(zs[0, r, lanes], zs[1, r, lanes]) for r in rows]
                for j in range(GROUP):
                    p = 2 * (GROUP * g + j)
                    parts = []
                    for (zre, zim), r in zip(z, rows):
                        cre, cim = pairs[p, r, lanes], pairs[p + 1, r, lanes]
                        parts.append((cre * zre - cim * zim, cre * zim + cim * zre))
                    (re1, im1), (re2, im2) = parts
                    place = wide * j + lane
                    for put, even, odd in ((place, re1 + re2, im1 - im2), (place + LANES, im1 + im2, re2 - re1)):
                        for base, value in ((0, even), (FOLD, odd)):
                            xs[pl.ds(base + at, 16), put : put + 128] = value

        ts[...] = dot_high(w_ref[0], xs[...])

        @pl.loop(0, LPAD // 16)
        def _(i):
            at = pl.multiple_of(16 * i, 16)
            for lane in range(0, GROUP * wide, 256):
                lanes = slice(lane, lane + 256)
                hi, lo = split(ts[pl.ds(at, 16), lanes])
                ss[pl.ds(at, 16), lanes] = hi
                ss[pl.ds(LPAD + at, 16), lanes] = lo
                ss[pl.ds(2 * LPAD + at, 16), lanes] = hi

        ys[...] = dot(ah_ref[0], ss[...])

        @pl.loop(0, FOLD // 8)
        def _(i):
            at = pl.multiple_of(8 * i, 8)
            rows = (pl.ds(at, 8), pl.ds(FOLD + at, 8))
            for lane in range(0, LANES, 128):
                lanes = slice(lane, lane + 128)
                sums = [None] * 4
                for j in range(GROUP):
                    p = 2 * (GROUP * g + j)
                    re = slice(wide * j + lane, wide * j + lane + 128)
                    im = slice(wide * j + LANES + lane, wide * j + LANES + lane + 128)
                    ure, uim, vre, vim = ys[rows[0], re], ys[rows[0], im], ys[rows[1], re], ys[rows[1], im]
                    for part, (yre, yim) in enumerate(((ure - vim, uim + vre), (ure + vim, uim - vre))):
                        cre, cim = pairs[p, rows[part], lanes], pairs[p + 1, rows[part], lanes]
                        for r, term in enumerate((cre * yre + cim * yim, cre * yim - cim * yre)):
                            old = sums[2 * part + r]
                            sums[2 * part + r] = term if old is None else old + term
                for part in range(2):
                    for r in range(2):
                        value = sums[2 * part + r]
                        acc[r, rows[part], lanes] = value + jnp.where(g > 0, acc[r, rows[part], lanes], 0.0)


def clear(*refs):
    @pl.when(pl.program_id(0) == 0)
    def _():
        for ref in refs:
            ref[...] = jnp.zeros_like(ref)


def first_kernel(pos_ref, base_ref, own_ref, mate_ref, got_ref, gotm_ref, e0, e1, e2, e3, w_ref, ah_ref,
                 u_ref, pairs, zs, zf, xs, ts, ss, ys, acc):
    planes = own_ref.shape[0]
    count = e0.shape[2]
    rows = count // HALF
    clear(pairs, zs, zf, xs, ss, acc)

    @pl.when(pl.program_id(0) == 0)
    def _():
        for part, (src, got) in enumerate(((own_ref, got_ref), (mate_ref, gotm_ref))):
            for k in range(planes):
                for half in range(2):

                    @pl.when(pos_ref[0] == half)
                    def _():
                        pairs[planes * part + k, :, :HALF] = src[k, :, HALF * half : HALF * (half + 1)]

                for fold in range(2):
                    pairs[planes * part + k, FOLD * fold : FOLD * fold + LINK, HALF : 2 * HALF] = got[
                        LINK * fold : LINK * (fold + 1), HALF * k : HALF * (k + 1)
                    ]

    for k, piece in enumerate((e0, e1, e2, e3)):
        start = rows * ((2 * pos_ref[0] + pos_ref[1]) ^ k)
        for row in range(rows):
            seg = piece[0, :, HALF * row : HALF * (row + 1)]
            y = start + row
            at = jnp.where(y <= NY // 2, y, FOLD + NY - y)
            for r in range(2):
                zf[r, pl.ds(at, 1), :] = seg[r : r + 1]
    for r in range(2):
        zs[r, :, :HALF] = zf[r]
        zs[r, :, HALF : 2 * HALF] = zf[r]
    normal(pairs, zs, w_ref, ah_ref, xs, ts, ss, ys, acc)
    for r in range(2):
        u_ref[0, r] = zf[r] - 0.5 * (acc[r, :, :HALF] + acc[r, :, HALF : 2 * HALF])


def pair_scratch():
    return [
        pltpu.VMEM((2, ROWS, LANES), F32),
        pltpu.VMEM((2, ROWS, HALF), F32),
        pltpu.VMEM((ROWS, 2 * GROUP * LANES), F32),
        pltpu.VMEM((LPAD, 2 * GROUP * LANES), F32),
        pltpu.VMEM((BACK, 2 * GROUP * LANES), BF),
        pltpu.VMEM((ROWS, 2 * GROUP * LANES), F32),
        pltpu.VMEM((2, ROWS, LANES), F32),
    ]


def line_specs():
    return [
        pl.BlockSpec((1, LPAD, ROWS), lambda d, p, s: (s[0] + d, 0, 0)),
        pl.BlockSpec((1, ROWS, BACK), lambda d, p, s: (s[0] + d, 0, 0)),
    ]


def first_step(pos, base, own, mate, got, gotm, pieces, w, ah):
    planes = own.shape[0]
    dirs, _, count = pieces[0].shape
    piece = pl.BlockSpec((1, 2, count), lambda d, p, s: (d, 0, 0))
    return pl.pallas_call(
        first_kernel,
        grid_spec=pltpu.PrefetchScalarGridSpec(
            num_scalar_prefetch=2,
            grid=(dirs,),
            in_specs=[whole(own.shape)] * 2 + [whole(got.shape)] * 2 + [piece] * 4 + line_specs(),
            out_specs=[
                pl.BlockSpec((1, 2, ROWS, HALF), lambda d, p, s: (d, 0, 0, 0)),
                result((2 * planes, ROWS, LANES)),
            ],
            scratch_shapes=pair_scratch(),
        ),
        out_shape=[
            jax.ShapeDtypeStruct((dirs, 2, ROWS, HALF), F32),
            jax.ShapeDtypeStruct((2 * planes, ROWS, LANES), F32),
        ],
        compiler_params=params(46),
        cost_estimate=cost(9e9, 30e6),
        name="first_step",
    )(pos, base, own, mate, got, gotm, *pieces, w, ah)


def second_kernel(pos_ref, base_ref, u_ref, keep_ref, got_ref, pairs, w_ref, ah_ref, z_ref, zs, zf, xs, ts, ss, ys, acc):
    clear(zs, zf, xs, ss, acc)
    for k in range(got_ref.shape[1] // (2 * HALF)):

        @pl.when(pl.program_id(0) == k)
        def _():
            for r in range(2):
                for part in range(2):
                    at = slice(FOLD * part, FOLD * part + LINK)
                    got = got_ref[LINK * part : LINK * (part + 1), HALF * (2 * k + r) : HALF * (2 * k + r + 1)]
                    zf[r, at, :] = 0.5 * (keep_ref[0, r, at, :] + got)

    for r in range(2):
        z = u_ref[0, r] + zf[r]
        zs[r, :, :HALF] = z
        zs[r, :, HALF : 2 * HALF] = z
        zf[r] = z + zf[r]
    normal(pairs, zs, w_ref, ah_ref, xs, ts, ss, ys, acc)
    for r in range(2):
        z_ref[0, r] = zf[r] - 0.5 * (acc[r, :, :HALF] + acc[r, :, HALF : 2 * HALF])


def second_step(pos, base, u, keep, got, pairs, w, ah):
    dirs = u.shape[0]
    plane = pl.BlockSpec((1, 2, ROWS, HALF), lambda d, p, s: (d, 0, 0, 0))
    return pl.pallas_call(
        second_kernel,
        grid_spec=pltpu.PrefetchScalarGridSpec(
            num_scalar_prefetch=2,
            grid=(dirs,),
            in_specs=[plane, plane, whole(got.shape), whole(pairs.shape)] + line_specs(),
            out_specs=plane,
            scratch_shapes=pair_scratch(),
        ),
        out_shape=jax.ShapeDtypeStruct(u.shape, F32),
        compiler_params=params(36),
        cost_estimate=cost(9e9, 20e6),
        name="second_step",
    )(pos, base, u, keep, got, pairs, w, ah)


def chunk_size(dirs):
    return -(-(75 * HALF) // (dirs * 128)) * 128


def flat_kernel(size, z_ref, o_ref, flat):
    dirs = z_ref.shape[0]
    rows = NY // 4
    parts = o_ref.shape[0] // 4
    for p in range(4):
        for row in range(rows):
            for d in range(dirs):
                for r in range(2):
                    at = folded(rows * p + row)
                    flat[d, r : r + 1, HALF * row : HALF * (row + 1)] = z_ref[d, r, at : at + 1, :]
        for q in range(parts):
            o_ref[4 * q + p] = flat[:, :, size * q : size * (q + 1)]


def flat_chunks(z, parts):
    dirs = z.shape[0]
    size = chunk_size(parts)
    shape = (4 * parts, dirs, 2, size)
    return pl.pallas_call(
        functools.partial(flat_kernel, size),
        grid=(1,),
        in_specs=[whole(z.shape)],
        out_specs=result(shape),
        out_shape=jax.ShapeDtypeStruct(shape, F32),
        scratch_shapes=[pltpu.VMEM((dirs, 2, size * parts), F32)],
        compiler_params=params(16),
        cost_estimate=cost(1e6, 5e6),
        name="flat_chunks",
    )(z)


def denoise_kernel(x_ref, w1_ref, b1_ref, w2_ref, o_ref, xs):
    parts = x_ref.shape[0] // 4
    own, size = x_ref.shape[1], x_ref.shape[3]
    for q in range(parts):
        for y in range(2):
            for core in range(2):
                for d in range(own):
                    at = 4 * own * q + 2 * own * core + 2 * d
                    xs[at : at + 2, size * y : size * (y + 1)] = x_ref[4 * q + 2 * y + core, d]
    w1h, w1l = split(w1_ref[...])
    w2h, w2l = split(w2_ref[...])
    w1 = jnp.concatenate([w1h, w1h, w1l], axis=1)
    w2 = jnp.concatenate([w2h, w2h, w2l], axis=1)
    x = xs[...]
    hi, lo = split(x)
    hidden = dot(w1, jnp.concatenate([hi, lo, hi], axis=0)) + b1_ref[...]
    hi, lo = split(jnp.maximum(hidden, 0.0))
    noise = dot(w2, jnp.concatenate([hi, lo, hi], axis=0))
    xs[...] = x - 0.5 * noise
    for q in range(parts):
        for d in range(2 * own):
            at = 4 * own * q + 2 * d
            o_ref[q, d] = xs[at : at + 2, :]


def denoise(x, w1, b1, w2):
    parts, own, size = x.shape[0] // 4, x.shape[1], x.shape[3]
    shape = (parts, 2 * own, 2, 2 * size)
    return pl.pallas_call(
        denoise_kernel,
        grid=(1,),
        in_specs=[whole(x.shape), whole(w1.shape), whole(b1.shape), whole(w2.shape)],
        out_specs=result(shape),
        out_shape=jax.ShapeDtypeStruct(shape, F32),
        scratch_shapes=[pltpu.VMEM((4 * own * parts, 2 * size), F32)],
        compiler_params=params(24),
        cost_estimate=cost(1e9, 3e6),
        name="denoise",
    )(x, w1, b1, w2)


def rows_kernel(x_ref, o_ref, flat):
    parts, size = x_ref.shape[0], x_ref.shape[3] // 2
    rows = o_ref.shape[2] // NX
    for half in range(2):
        for q in range(parts):
            flat[:, :, size * q : size * (q + 1)] = x_ref[q, :, :, size * half : size * (half + 1)]
        for row in range(rows):
            at = NX * row + HALF * half
            o_ref[:, :, at : at + HALF] = flat[:, :, HALF * row : HALF * (row + 1)]


def flat_rows(x, count):
    parts, dirs, _, size = x.shape
    return pl.pallas_call(
        rows_kernel,
        grid=(1,),
        in_specs=[whole(x.shape)],
        out_specs=result((dirs, 2, count)),
        out_shape=jax.ShapeDtypeStruct((dirs, 2, count), F32),
        scratch_shapes=[pltpu.VMEM((dirs, 2, parts * size // 2), F32)],
        compiler_params=params(16),
        cost_estimate=cost(1e6, 3e6),
        name="flat_rows",
    )(x)


def paired(estimate, coil_maps, kspace, lines, first_weight, first_bias, second_weight):
    dirs, _, share = estimate.shape
    own_dirs = dirs // 2
    coils = coil_maps.shape[0]
    parts = lax.axis_size("dir")
    back, rows = host_tables()
    high, low = split_host(back)
    f_back = jnp.asarray(np.concatenate([high, low]))
    index = lax.axis_index("coil")
    pos = jnp.stack([index // 2, index % 2]).astype(jnp.int32)
    mine = (own_dirs * pos[1:2]).astype(jnp.int32)

    def swap(value, k):
        return lax.ppermute(value, "coil", [(p, p ^ k) for p in range(4)])

    k_own = kspace.transpose(0, 1, 2, 4, 3, 5).reshape(dirs, 2 * coils, kspace.shape[4], 1, NX)
    maps, half = folded_maps(pos, coil_maps.reshape(2 * coils, 1, NY, NX).transpose(0, 2, 1, 3))
    mate = swap(maps, 1)
    k_mate = swap(k_own, 1)
    pieces = estimate_pieces(pos, estimate)
    pieces = [pieces[k] if k == 0 else swap(pieces[k], k) for k in range(4)]
    got = swap(half, 2)
    w, ah = line_matrices(lines, rows)
    keep, send = back_sums(mine, pos, own_dirs, k_own, k_mate, maps, mate, f_back, ah)
    send, got, *pieces = lax.optimization_barrier((send, got, *pieces))
    got_b = swap(send, 2)
    gotm = swap(got, 1)
    u, pairs = first_step(pos, mine, maps, mate, got, gotm, pieces, w, ah)
    z = second_step(pos, mine, u, keep, got_b, pairs, w, ah)
    chunks = flat_chunks(z, parts)
    received = lax.all_to_all(chunks, ("dir", "coil"), split_axis=0, concat_axis=0, tiled=True)
    channels = first_bias.shape[0]
    w1 = first_weight.reshape(-1, channels).T
    w2 = second_weight.reshape(channels, -1).T
    result = denoise(received, w1, first_bias[:, None], w2)
    returned = lax.all_to_all(result, "dir", split_axis=0, concat_axis=0, tiled=True)
    return flat_rows(returned, share)


def transform_rows(index, length):
    columns = jnp.arange(length, dtype=jnp.int32)
    product = index[:, None] * columns[None, :] % length
    angle = 2.0 * math.pi / length * product.astype(jnp.float32)
    scale = 1.0 / math.sqrt(length)
    return (jnp.cos(angle) * scale, -jnp.sin(angle) * scale)


def data_gradient(image, coil_maps, kspace, chosen, cols_cos, cols_sin):
    highest = lax.Precision.HIGHEST
    lines_cos, lines_sin = transform_rows(chosen, NY)
    coil_real, coil_imag = (coil_maps[:, 0], coil_maps[:, 1])
    image_real, image_imag = (image[0][None], image[1][None])
    prod_real = coil_real * image_real - coil_imag * image_imag
    prod_imag = coil_real * image_imag + coil_imag * image_real
    rows_form = "ly,csyx->cslx"
    half_real = jnp.einsum(rows_form, lines_cos, prod_real, precision=highest) - jnp.einsum(
        rows_form, lines_sin, prod_imag, precision=highest
    )
    half_imag = jnp.einsum(rows_form, lines_cos, prod_imag, precision=highest) + jnp.einsum(
        rows_form, lines_sin, prod_real, precision=highest
    )
    cols_form = "cslx,xk->cslk"
    pred_real = jnp.einsum(cols_form, half_real, cols_cos, precision=highest) - jnp.einsum(
        cols_form, half_imag, cols_sin, precision=highest
    )
    pred_imag = jnp.einsum(cols_form, half_real, cols_sin, precision=highest) + jnp.einsum(
        cols_form, half_imag, cols_cos, precision=highest
    )
    diff_real = pred_real - kspace[:, 0]
    diff_imag = pred_imag - kspace[:, 1]
    back_real = jnp.einsum(cols_form, diff_real, cols_cos, precision=highest) + jnp.einsum(
        cols_form, diff_imag, cols_sin, precision=highest
    )
    back_imag = jnp.einsum(cols_form, diff_imag, cols_cos, precision=highest) - jnp.einsum(
        cols_form, diff_real, cols_sin, precision=highest
    )
    adjoint_form = "ly,cslx->csyx"
    spread_real = jnp.einsum(adjoint_form, lines_cos, back_real, precision=highest) + jnp.einsum(
        adjoint_form, lines_sin, back_imag, precision=highest
    )
    spread_imag = jnp.einsum(adjoint_form, lines_cos, back_imag, precision=highest) - jnp.einsum(
        adjoint_form, lines_sin, back_real, precision=highest
    )
    grad_real = jnp.sum(coil_real * spread_real + coil_imag * spread_imag, axis=0)
    grad_imag = jnp.sum(coil_real * spread_imag - coil_imag * spread_real, axis=0)
    return jnp.stack([grad_real, grad_imag])


def per_device(estimate, coil_maps, kspace, lines, first_weight, first_bias, second_weight):
    highest = lax.Precision.HIGHEST
    dir_local = estimate.shape[0]
    share = estimate.shape[2]
    voxels = SLICES * NY * NX
    cols_cos, cols_sin = transform_rows(jnp.arange(NX, dtype=jnp.int32), NX)
    whole = lax.all_gather(estimate, "coil", axis=2, tiled=True)
    position = lax.axis_index("coil")
    current = whole
    for step in range(INNER):
        image = current.reshape(dir_local, 2, SLICES, NY, NX)

        def one_direction(item):
            return data_gradient(item[0], coil_maps, item[1], item[2], cols_cos, cols_sin)

        terms = lax.map(one_direction, (image, kspace, lines))
        total = lax.psum(terms.reshape(dir_local, 2, voxels), "coil")
        current = current - 0.5 * total
    own = lax.dynamic_slice_in_dim(current, position * share, share, 2)
    groups = lax.axis_size("dir")
    padded_len = -(-share // groups) * groups
    padded = jnp.pad(own, ((0, 0), (0, 0), (0, padded_len - share)))
    gathered = lax.all_to_all(padded, "dir", split_axis=2, concat_axis=0, tiled=True)
    hidden = (
        jnp.einsum("drv,drh->hv", gathered, first_weight, precision=highest) + first_bias[:, None]
    )
    hidden = jnp.maximum(hidden, 0.0)
    noise = jnp.einsum("hv,hdr->drv", hidden, second_weight, precision=highest)
    returned = lax.all_to_all(noise, "dir", split_axis=0, concat_axis=2, tiled=True)
    return own - 0.5 * returned[:, :, :share]


def chosen(*arrays):
    estimate, coil_maps, kspace = arrays[:3]
    fits = (
        lax.axis_size("coil") == 4
        and estimate.shape[0] % 2 == 0
        and estimate.shape[2] * 4 == NY * NX
        and coil_maps.shape[0] % 2 == 0
        and kspace.shape[4] <= LPAD
    )
    return paired(*arrays) if fits else per_device(*arrays)


def solution(mesh):
    return jax.shard_map(
        chosen,
        mesh=mesh,
        in_specs=(
            P("dir", None, "coil"),
            P("coil", None, None, None, None),
            P("dir", "coil", None, None, None, None),
            P("dir", None),
            P(),
            P(),
            P(),
        ),
        out_specs=P("dir", None, "coil"),
        check_vma=False,
    )
```

time: 232 us -> 202 us (0.87)
  local copies, waits for them, and re-layouts: 29.8 us -> 7.55 us
  Pallas kernels: 130 us -> 113 us
  waiting for transfers between devices: 25.3 us -> 33.3 us
  starting transfers between devices: 14.1 us -> 16.6 us
    pallas_call x4 -> x2, Pallas kernels: 39.6 us -> 32.8 us  [the longest x1 29.1 us: back_sums(): pl.pallas_call(back_kernel, grid_spec=pltpu.PrefetchScalarGridSpec(num_sc...]
    ppermute x8, waiting for transfers between devices: 0.02 us -> 6.62 us  [swap(): return lax.ppermute(value, 'coil', [(p, p ^ k) for p in range(4)])]
    ppermute x2 -> x0, local copies, waits for them, and re-layouts: 6.09 us -> none  [swap(): return lax.ppermute(value, 'coil', [(p, p ^ k) for p in range(4)])]
    pallas_call x1 -> x0, local copies, waits for them, and re-layouts: 5.02 us -> none  [back_partial(): pl.pallas_call(back_kernel, grid_spec=pltpu.PrefetchScalarGridSpec(num_sc...]
    unnamed x14 -> x22, local copies, waits for them, and re-layouts: 10.9 us -> 7.22 us
    pallas_call x1, Pallas kernels: 9.33 us -> 5.75 us  [line_matrices(): pl.pallas_call(lines_kernel, grid=(dirs,), in_specs=[pl.BlockSpec((1, LPA...]
    reshape x1 -> x0, local copies, waits for them, and re-layouts: 2.95 us -> none  [paired(): maps = coil_maps.reshape(2 * coils, NY, NX)]
    ppermute x8, starting transfers between devices: 5.64 us -> 8.33 us  [swap(): return lax.ppermute(value, 'coil', [(p, p ^ k) for p in range(4)])]
  transfers between devices with their start and end apart: 9 -> 9, of which waited for: 1 -> 4; matrix products, arithmetic and copies ran while one was open for 11% -> 0% of each run, Pallas kernels for 36% -> 39%
where the time goes in v2:
time: 202 us
  Pallas kernels  113 us (56%)
  waiting for transfers between devices  33.3 us (16%)
  blocking collectives  30.9 us (15%)
  starting transfers between devices  16.6 us (8%)
  local copies, waits for them, and re-layouts  7.55 us (4%)
    pallas_call x1, Pallas kernels, first_step(): pl.pallas_call(first_kernel, grid_spec=pltpu.PrefetchScalarGridSpec(num_s...  38.3 us
    all_to_all x1, blocking collectives, paired(): lax.all_to_all(result, 'dir', split_axis=0, concat_axis=0, tiled=True)  30.9 us
    pallas_call x1, Pallas kernels, back_sums(): pl.pallas_call(back_kernel, grid_spec=pltpu.PrefetchScalarGridSpec(num_sc...  29.1 us
    pallas_call x1, Pallas kernels, second_step(): pl.pallas_call(second_kernel, grid_spec=pltpu.PrefetchScalarGridSpec(num_...  27.3 us
    all_to_all x1, waiting for transfers between devices, paired(): lax.all_to_all(chunks, ('dir', 'coil'), split_axis=0, concat_axis=0, tile...  26.7 us
    ppermute x8, starting transfers between devices, swap(): return lax.ppermute(value, 'coil', [(p, p ^ k) for p in range(4)])  8.33 us
    all_to_all x1, starting transfers between devices, paired(): lax.all_to_all(chunks, ('dir', 'coil'), split_axis=0, concat_axis=0, tile...  8.32 us
    unnamed x22, local copies, waits for them, and re-layouts  7.22 us
  transfers between devices with their start and end apart: 9, of which 4 were waited for; matrix products, arithmetic and copies ran while one was open for 0% of the time, Pallas kernels for 39%

profile of v2, /device:TPU:0, one launch (start us, length us, event | category | flops | bytes accessed | tf_op | source)
XLA Modules:
  0.0 201.9 jit_solution(4288641377123123550)
XLA Ops:
  0.0 0.5 collective-permute-start.1
  0.5 2.0 %copy-done.2 = f32[4,2,1,300,300]{4,2,3,1,0:T(1,128)S(1)} copy-done((f32[4,2,1,300,300]{4,2,3,1,0:T(1,128)S(1)}, f32[4,2,1,300,300]{4,2,3,1,0:T(1,128)}, u32[]{:S(2)}) %copy-start.2) | copy-done | bytes 2880024
  2.6 3.7 %folded_maps.1 = (f32[8,320,384]{2,1,0:T(8,128)S(1)}, f32[304,1200]{1,0:T(8,128)}) custom-call(s32[2]{0:T(128)S(1)} %pad_add_fusion.pos_ref, f32[8,300,1,300]{3,2,1,0:T(1,128)S(1)} %bitcast.12), custom_call_target="tpu_custom_call" | custom-call | flops 1000 | bytes 12000 | tf_op jit(solution)/shard_map/folded_maps/pallas_call | solution.py:140
  6.3 1.9 copy-done
  8.3 3.0 %collective-permute-start.2 = (f32[304,1200]{1,0:T(8,128)}, f32[304,1200]{1,0:T(8,128)S(1)}, u32[]{:S(2)}, u32[]{:S(2)}) collective-permute-start(f32[304,1200]{1,0:T(8,128)} %get-tuple-element.26), channel_id=1, source_target_pairs={{0,2},{1,3},{2,0},{3,1},{4,6},{5,7},{6,4},{7,5},{8,10},{9,11},{10,... | collective-permute-start | bytes 4377608 | tf_op jit(solution)/shard_map/ppermute | solution.py:600
  11.3 2.4 %estimate_pieces.1 = (f32[3,2,11250]{2,1,0:T(2,128)S(1)}, f32[3,2,11250]{2,1,0:T(2,128)}, f32[3,2,11250]{2,1,0:T(2,128)}, f32[3,2,11250]{2,1,0:T(2,128)}) custom-call(s32[2]{0:T(128)S(1)} %pad_add_fusion.pos_ref, f32[6,2,22500]{2,1,0:T(2,128)S(1)} %copy-done.3), custom_call_target="tpu_custom_call" | custom-call | flops 1000 | bytes 8000 | tf_op jit(solution)/shard_map/estimate_pieces/pallas_call | solution.py:173
  13.7 1.3 collective-permute-done.c1_ref.mate_ref
  15.0 2.6 %collective-permute-start.5 = (f32[3,2,11250]{2,1,0:T(2,128)}, f32[3,2,11250]{2,1,0:T(2,128)}, u32[]{:S(2)}, u32[]{:S(2)}) collective-permute-start(f32[3,2,11250]{2,1,0:T(2,128)} %get-tuple-element.30), channel_id=1, source_target_pairs={{0,3},{1,2},{2,1},{3,0},{4,7},{5,6},{6,5},{7,4},{8,11},{9,10},{10,... | collective-permute-start | bytes 810008 | tf_op jit(solution)/shard_map/ppermute | solution.py:600
  17.7 0.1 copy.13.lines_ref
  17.8 5.7 %line_matrices.1 = (f32[6,80,320]{2,1,0:T(8,128)S(1)}, bf16[6,320,256]{2,1,0:T(8,128)(2,1)S(1)}) custom-call(s32[6,80,1]{2,1,0:T(8,128)S(1)} %copy.13.lines_ref, f32[300,320]{1,0:T(8,128)S(1)} %copy-done.5, f32[320,300]{1,0:T(8,128)S(1)} %copy-done.4), custom_call_target="tpu_custom_call" | custom-call | flops 1000000 | bytes 1000 | tf_op jit(solution)/shard_map/line_matrices/pallas_call | solution.py:97
  23.6 29.1 %back_sums.1 = (f32[3,2,320,150]{3,2,1,0:T(8,128)S(1)}, f32[304,900]{1,0:T(8,128)S(1)}) custom-call(s32[1]{0:T(128)S(6)} %mul.3.base_ref, s32[2]{0:T(128)S(1)} %pad_add_fusion.pos_ref, f32[6,8,75,1,300]{4,3,2,1,0:T(1,128)} %bitcast.16, f32[6,8,75,1,300]{4,3,2,1,0:T(1,128)} %collective-permute-done.1.k1_ref, f32[8,320,384]{2,1,0:T(8,128)} %copy-done, ...), custom_call_target="tpu_custom_call" | custom-call | flops 14000000 | bytes 22000 | tf_op jit(solution)/shard_map/back_sums/pallas_call | solution.py:268
  52.7 4.0 %collective-permute-done.5.e3 = f32[3,2,11250]{2,1,0:T(2,128)} collective-permute-done((f32[3,2,11250]{2,1,0:T(2,128)}, f32[3,2,11250]{2,1,0:T(2,128)}, u32[]{:S(2)}, u32[]{:S(2)}) %collective-permute-start.5) | collective-permute-done | bytes 270032 | tf_op jit(solution)/shard_map/ppermute | solution.py:600
  56.7 0.5 collective-permute-start.6
  57.2 1.7 collective-permute-start.7
  58.9 1.3 collective-permute-done.6.gotm_ref
  60.2 38.3 %first_step.1 = (f32[3,2,320,150]{3,2,1,0:T(8,128)S(1)}, f32[16,320,384]{2,1,0:T(8,128)}) custom-call(s32[2]{0:T(128)S(1)} %pad_add_fusion.pos_ref, s32[1]{0:T(128)S(6)} %mul.3.base_ref, f32[8,320,384]{2,1,0:T(8,128)} %copy-done, f32[8,320,384]{2,1,0:T(8,128)} %copy-done.7, f32[304,1200]{1,0:T(8,128)S(1)} %collective-permute-done.2.got_ref, ...), custom_call_target="tpu_custom_call" | custom-call | flops 9000000 | bytes 30000 | tf_op jit(solution)/shard_map/first_step/pallas_call | solution.py:422
  98.6 3.2 %copy-done.1 = f32[16,320,384]{2,1,0:T(8,128)S(1)} copy-done((f32[16,320,384]{2,1,0:T(8,128)S(1)}, f32[16,320,384]{2,1,0:T(8,128)}, u32[]{:S(2)}) %copy-start.1) | copy-done | bytes 7864344
  101.8 27.3 %second_step.1.z_ref = f32[3,2,320,150]{3,2,1,0:T(8,128)S(1)} custom-call(s32[2]{0:T(128)S(1)} %pad_add_fusion.pos_ref, s32[1]{0:T(128)S(6)} %mul.3.base_ref, f32[3,2,320,150]{3,2,1,0:T(8,128)S(1)} %get-tuple-element.37.u_ref, f32[3,2,320,150]{3,2,1,0:T(8,128)S(1)} %get-tuple-element.38.keep_ref, f32[304,900]{1,0:T(8,128)S(1)} %collective-permute-done.7.got_ref, ...), custom_call_target="tpu_custom_call" | custom-call | flops 9000000 | bytes 20000 | tf_op jit(solution)/shard_map/second_step/pallas_call | solution.py:469
  129.1 3.2 %flat_chunks.1 = f32[32,3,2,1408]{3,2,1,0:T(2,128)} custom-call(f32[3,2,320,150]{3,2,1,0:T(8,128)S(1)} %second_step.1.z_ref), custom_call_target="tpu_custom_call" | custom-call | flops 1000 | bytes 5000 | tf_op jit(solution)/shard_map/flat_chunks/pallas_call | solution.py:507
  132.3 8.3 %all-to-all-start = ((f32[32,3,2,1408]{3,2,1,0:T(2,128)}), f32[32,3,2,1408]{3,2,1,0:T(2,128)S(1)}, u32[]{:S(2)}, u32[]{:S(2)}) async-start(f32[32,3,2,1408]{3,2,1,0:T(2,128)} %flat_chunks.1), calls=%async_computation | async-start | bytes 2162688 | tf_op jit(solution)/shard_map/all_to_all | solution.py:617
  140.9 26.7 %all-to-all-done.x_ref = f32[32,3,2,1408]{3,2,1,0:T(2,128)S(1)} async-done(((f32[32,3,2,1408]{3,2,1,0:T(2,128)}), f32[32,3,2,1408]{3,2,1,0:T(2,128)S(1)}, u32[]{:S(2)}, u32[]{:S(2)}) %all-to-all-start) | async-done | bytes 1081376 | tf_op jit(solution)/shard_map/all_to_all | solution.py:617
  167.6 1.4 denoise.1
  169.0 30.9 %all_to_all.10.x_ref = f32[8,6,2,2816]{3,2,1,0:T(2,128)S(1)} all-to-all(f32[8,6,2,2816]{3,2,1,0:T(2,128)S(1)} %denoise.1), channel_id=1, replica_groups=mesh['dir'=8,'coil'=4] {'dir'}, dimensions={0} | all-to-all | bytes 2162688 | tf_op jit(solution)/shard_map/all_to_all | solution.py:622
  199.9 2.0 %flat_rows.1 = f32[6,2,22500]{2,1,0:T(2,128)} custom-call(f32[8,6,2,2816]{3,2,1,0:T(2,128)S(1)} %all_to_all.10.x_ref), custom_call_target="tpu_custom_call" | custom-call | flops 1000 | bytes 3000 | tf_op jit(solution)/shard_map/flat_rows/pallas_call | solution.py:574
  (31 shorter events, 0.4 us)
Async XLA Ops:
  0.0 23.6 %collective-permute-start.1 = (f32[6,8,75,1,300]{4,3,2,1,0:T(1,128)}, f32[6,8,75,1,300]{4,3,2,1,0:T(1,128)}, u32[]{:S(2)}, u32[]{:S(2)}) collective-permute-start(f32[6,8,75,1,300]{4,3,2,1,0:T(1,128)} %bitcast.15), channel_id=1, source_target_pairs={{0,1},{1,0},{2,3},{3,2},{4,5},{5,4},{6,7},{7,6},{8,9},{9,8},{10,11... | collective-permute-start | bytes 12960008 | tf_op jit(solution)/shard_map/ppermute | solution.py:600
  0.5 2.0 %copy-start.2 = (f32[4,2,1,300,300]{4,2,3,1,0:T(1,128)S(1)}, f32[4,2,1,300,300]{4,2,3,1,0:T(1,128)}, u32[]{:S(2)}) copy-start(f32[4,2,1,300,300]{4,2,3,1,0:T(1,128)} %param.11) | copy-start | bytes 8640004
  2.6 8.7 %copy-start.3 = (f32[6,2,22500]{2,1,0:T(2,128)S(1)}, f32[6,2,22500]{2,1,0:T(2,128)}, u32[]{:S(2)}) copy-start(f32[6,2,22500]{2,1,0:T(2,128)} %est_ref.1) | copy-start | bytes 3240004
  2.6 15.1 %copy-start.9 = (s32[6,75]{1,0:T(8,128)S(1)}, s32[6,75]{1,0:T(8,128)}, u32[]{:S(2)}) copy-start(s32[6,75]{1,0:T(8,128)} %param.13) | copy-start | bytes 5404
  6.3 1.9 copy-start
  6.3 11.5 %copy-start.4 = (f32[320,300]{1,0:T(8,128)S(1)}, f32[320,300]{1,0:T(8,128)}, u32[]{:S(2)}) copy-start(f32[320,300]{1,0:T(8,128)} %constant.39.clone.cols_ref) | copy-start | bytes 1152004
  6.3 11.5 %copy-start.5 = (f32[300,320]{1,0:T(8,128)S(1)}, f32[300,320]{1,0:T(8,128)}, u32[]{:S(2)}) copy-start(f32[300,320]{1,0:T(8,128)} %constant.38.clone.rows_ref) | copy-start | bytes 1152004
  8.2 6.8 %collective-permute-start = (f32[8,320,384]{2,1,0:T(8,128)S(1)}, f32[8,320,384]{2,1,0:T(8,128)S(1)}, u32[]{:S(2)}, u32[]{:S(2)}) collective-permute-start(f32[8,320,384]{2,1,0:T(8,128)S(1)} %get-tuple-element.23.c0_ref.own_ref), channel_id=1, source_target_pairs={{0,1},{1,0},{2,3},{3,2},{4,5},{5,4},{6,7},{7,6},{8,9},{9,8},{10,11... | collective-permute-start | bytes 11796488 | tf_op jit(solution)/shard_map/ppermute | solution.py:600
  8.3 48.4 %collective-permute-start.2 = (f32[304,1200]{1,0:T(8,128)}, f32[304,1200]{1,0:T(8,128)S(1)}, u32[]{:S(2)}, u32[]{:S(2)}) collective-permute-start(f32[304,1200]{1,0:T(8,128)} %get-tuple-element.26), channel_id=1, source_target_pairs={{0,2},{1,3},{2,0},{3,1},{4,6},{5,7},{6,4},{7,5},{8,10},{9,11},{10,... | collective-permute-start | bytes 4377608 | tf_op jit(solution)/shard_map/ppermute | solution.py:600
  13.7 39.0 %collective-permute-start.3 = (f32[3,2,11250]{2,1,0:T(2,128)}, f32[3,2,11250]{2,1,0:T(2,128)S(1)}, u32[]{:S(2)}, u32[]{:S(2)}) collective-permute-start(f32[3,2,11250]{2,1,0:T(2,128)} %get-tuple-element.28), channel_id=1, source_target_pairs={{0,1},{1,0},{2,3},{3,2},{4,5},{5,4},{6,7},{7,6},{8,9},{9,8},{10,11... | collective-permute-start | bytes 810008 | tf_op jit(solution)/shard_map/ppermute | solution.py:600
  13.7 39.0 %collective-permute-start.4 = (f32[3,2,11250]{2,1,0:T(2,128)}, f32[3,2,11250]{2,1,0:T(2,128)}, u32[]{:S(2)}, u32[]{:S(2)}) collective-permute-start(f32[3,2,11250]{2,1,0:T(2,128)} %get-tuple-element.29), channel_id=1, source_target_pairs={{0,2},{1,3},{2,0},{3,1},{4,6},{5,7},{6,4},{7,5},{8,10},{9,11},{10,... | collective-permute-start | bytes 810008 | tf_op jit(solution)/shard_map/ppermute | solution.py:600
  15.0 2.6 %copy-start.7 = (f32[8,320,384]{2,1,0:T(8,128)}, f32[8,320,384]{2,1,0:T(8,128)S(1)}, u32[]{:S(2)}) copy-start(f32[8,320,384]{2,1,0:T(8,128)S(1)} %collective-permute-done.c1_ref.mate_ref) | copy-start | bytes 11796484
  15.0 41.7 %collective-permute-start.5 = (f32[3,2,11250]{2,1,0:T(2,128)}, f32[3,2,11250]{2,1,0:T(2,128)}, u32[]{:S(2)}, u32[]{:S(2)}) collective-permute-start(f32[3,2,11250]{2,1,0:T(2,128)} %get-tuple-element.30), channel_id=1, source_target_pairs={{0,3},{1,2},{2,1},{3,0},{4,7},{5,6},{6,5},{7,4},{8,11},{9,10},{10,... | collective-permute-start | bytes 810008 | tf_op jit(solution)/shard_map/ppermute | solution.py:600
  56.7 3.5 %collective-permute-start.6 = (f32[304,1200]{1,0:T(8,128)S(1)}, f32[304,1200]{1,0:T(8,128)S(1)}, u32[]{:S(2)}, u32[]{:S(2)}) collective-permute-start(f32[304,1200]{1,0:T(8,128)S(1)} %collective-permute-done.2.got_ref), channel_id=1, source_target_pairs={{0,1},{1,0},{2,3},{3,2},{4,5},{5,4},{6,7},{7,6},{8,9},{9,8},{10,11... | collective-permute-start | bytes 4377608 | tf_op jit(solution)/shard_map/ppermute | solution.py:600
  57.2 41.4 %collective-permute-start.7 = (f32[304,900]{1,0:T(8,128)S(1)}, f32[304,900]{1,0:T(8,128)S(1)}, u32[]{:S(2)}, u32[]{:S(2)}) collective-permute-start(f32[304,900]{1,0:T(8,128)S(1)} %get-tuple-element.39), channel_id=1, source_target_pairs={{0,2},{1,3},{2,0},{3,1},{4,6},{5,7},{6,4},{7,5},{8,10},{9,11},{10,... | collective-permute-start | bytes 3283208 | tf_op jit(solution)/shard_map/ppermute | solution.py:600
  98.6 3.2 %copy-start.1 = (f32[16,320,384]{2,1,0:T(8,128)S(1)}, f32[16,320,384]{2,1,0:T(8,128)}, u32[]{:S(2)}) copy-start(f32[16,320,384]{2,1,0:T(8,128)} %get-tuple-element.40.pairs) | copy-start | bytes 23592964
  132.3 8.3 %copy-start.8 = (f32[48,2,96]{2,1,0:T(2,128)S(1)}, f32[48,2,96]{2,1,0:T(2,128)}, u32[]{:S(2)}) copy-start(f32[48,2,96]{2,1,0:T(2,128)} %param.14) | copy-start | bytes 110596
  132.3 8.4 %copy-start.10 = (f32[96]{0:T(128)S(1)}, f32[96]{0:T(128)}, u32[]{:S(2)}) copy-start(f32[96]{0:T(128)} %param.15) | copy-start | bytes 1156
  132.3 35.3 %copy-start.6 = (f32[96,48,2]{0,2,1:T(2,128)S(1)}, f32[96,48,2]{0,2,1:T(2,128)}, u32[]{:S(2)}) copy-start(f32[96,48,2]{0,2,1:T(2,128)} %param.16) | copy-start | bytes 110596
  132.3 35.3 %all-to-all-start = ((f32[32,3,2,1408]{3,2,1,0:T(2,128)}), f32[32,3,2,1408]{3,2,1,0:T(2,128)S(1)}, u32[]{:S(2)}, u32[]{:S(2)}) async-start(f32[32,3,2,1408]{3,2,1,0:T(2,128)} %flat_chunks.1), calls=%async_computation | async-start | bytes 2162688 | tf_op jit(solution)/shard_map/all_to_all | solution.py:617

commit v3 on v2

--- a/solution.py
+++ b/solution.py
@@ -23,7 +23,7 @@
 LPAD = 80
 HALF = 150
 BACK = 256
-GROUP = 4
+GROUP = 2
 
 
 def split_host(table):
@@ -192,55 +192,53 @@
     return ((rows, ure - vim, uim + vre), (mirror, ure + vim, uim - vre))
 
 
-def back_kernel(base_ref, pos_ref, k0_ref, k1_ref, c0_ref, c1_ref, f_ref, ah_ref, keep_ref, send_ref, xs, ts, ss, ys, bs):
+def back_kernel(base_ref, pos_ref, k0_ref, k1_ref, c0_ref, c1_ref, f_ref, ah_ref, keep_ref, send_ref, xs, ss, ys, bs):
     coils = c0_ref.shape[0] // 2
     count = k0_ref.shape[2]
     wide = 2 * LANES
-    sources = [(k, m, c) for k, m in ((k0_ref, c0_ref), (k1_ref, c1_ref)) for c in range(coils)]
 
     @pl.when(pl.program_id(0) == 0)
     def _():
         xs[...] = jnp.zeros_like(xs)
         ss[...] = jnp.zeros_like(ss)
 
-    for part, k_ref in enumerate((k0_ref, k1_ref)):
-
-        @pl.loop(0, coils)
-        def _(c):
-            base = pl.multiple_of(LPAD * (coils * part + c), LPAD)
+    def load(part, k_ref):
+        for c in range(coils):
             for r in range(2):
-                xs[pl.ds(base, count), LANES * r : LANES * r + NX] = k_ref[0, 2 * c + r, :, 0, :]
-
-    hi, lo = split(xs[...])
-    ts[...] = dot(hi, f_ref[:wide]) + dot(lo, f_ref[:wide]) + dot(hi, f_ref[wide:])
-
-    @pl.loop(0, LPAD // 16)
-    def _(i):
-        at = pl.multiple_of(16 * i, 16)
-        for c in range(len(sources)):
-            for lane in range(0, wide, 256):
-                hi, lo = split(ts[pl.ds(LPAD * c + at, 16), lane : lane + 256])
-                lanes = slice(wide * c + lane, wide * c + lane + 256)
-                ss[pl.ds(at, 16), lanes] = hi
-                ss[pl.ds(LPAD + at, 16), lanes] = lo
-                ss[pl.ds(2 * LPAD + at, 16), lanes] = hi
-
-    ys[...] = dot(ah_ref[0], ss[...])
-
-    @pl.loop(0, FOLD // 8)
-    def _(i):
-        rows = pl.ds(pl.multiple_of(8 * i, 8), 8)
-        sums = [None] * 4
-        for place, (_, c_ref, c) in enumerate(sources):
-            for part, (at, yre, yim) in enumerate(adjoint(ys, place, rows)):
-                cre, cim = c_ref[2 * c, at], c_ref[2 * c + 1, at]
-                for r, term in enumerate((cre * yre + cim * yim, cre * yim - cim * yre)):
-                    old = sums[2 * part + r]
-                    sums[2 * part + r] = term if old is None else old + term
-        for part in range(2):
-            for r in range(2):
-                bs[r, pl.ds(pl.multiple_of(FOLD * part + 8 * i, 8), 8), :] = sums[2 * part + r]
-
+                xs[part, LPAD * c : LPAD * c + count, LANES * r : LANES * r + NX] = k_ref[0, 2 * c + r, :, 0, :]
+
+    def multiply(part):
+        hi, lo = split(xs[part])
+        t = dot(hi, f_ref[:wide]) + dot(lo, f_ref[:wide]) + dot(hi, f_ref[wide:])
+        for c in range(coils):
+            hi, lo = split(t[LPAD * c : LPAD * (c + 1)])
+            lanes = slice(wide * c, wide * (c + 1))
+            ss[part, :LPAD, lanes] = hi
+            ss[part, LPAD : 2 * LPAD, lanes] = lo
+            ss[part, 2 * LPAD : 3 * LPAD, lanes] = hi
+        ys[part] = dot(ah_ref[0], ss[part])
+
+    def gather(part, c_ref):
+        for start in range(0, FOLD, 8):
+            sums = [None] * 4
+            if part > 0:
+                sums = [bs[r, FOLD * f + start : FOLD * f + start + 8] for f in range(2) for r in range(2)]
+            for c in range(coils):
+                for f, (at, yre, yim) in enumerate(adjoint(ys.at[part], c, pl.ds(start, 8))):
+                    cre, cim = c_ref[2 * c, at], c_ref[2 * c + 1, at]
+                    for r, term in enumerate((cre * yre + cim * yim, cre * yim - cim * yre)):
+                        old = sums[2 * f + r]
+                        sums[2 * f + r] = term if old is None else old + term
+            for f in range(2):
+                for r in range(2):
+                    bs[r, FOLD * f + start : FOLD * f + start + 8] = sums[2 * f + r]
+
+    load(0, k0_ref)
+    load(1, k1_ref)
+    multiply(0)
+    multiply(1)
+    gather(0, c0_ref)
+    gather(1, c1_ref)
     for half in range(2):
         lanes = slice(HALF * half, HALF * (half + 1))
 
@@ -275,10 +273,9 @@
             + [whole(f_back.shape), pl.BlockSpec((1, ROWS, BACK), lambda d, s, *_: (s[0] + d, 0, 0))],
             out_specs=[pl.BlockSpec((1, 2, ROWS, HALF), lambda d, *_: (d, 0, 0, 0)), result(link)],
             scratch_shapes=[
-                pltpu.VMEM((planes * LPAD, 2 * LANES), F32),
-                pltpu.VMEM((planes * LPAD, 2 * LANES), F32),
-                pltpu.VMEM((BACK, 2 * planes * LANES), BF),
-                pltpu.VMEM((ROWS, 2 * planes * LANES), F32),
+                pltpu.VMEM((2, planes // 2 * LPAD, 2 * LANES), F32),
+                pltpu.VMEM((2, BACK, planes * LANES), BF),
+                pltpu.VMEM((2, ROWS, planes * LANES), F32),
                 pltpu.VMEM((2, ROWS, LANES), F32),
             ],
         ),
@@ -289,16 +286,14 @@
     )(base, pos, k_own, k_mate, own, mate, f_back, ah)
 
 
-def normal(pairs, zs, w_ref, ah_ref, xs, ts, ss, ys, acc):
+def normal(pairs, zs, w_ref, ah_ref, xs, ss, ys, acc):
     groups = pairs.shape[0] // (2 * GROUP)
     wide = 2 * LANES
 
-    @pl.loop(0, groups)
-    def _(g):
-        @pl.loop(0, FOLD // 16)
-        def _(i):
-            at = pl.multiple_of(16 * i, 16)
-            rows = (pl.ds(at, 16), pl.ds(FOLD + at, 16))
+    def products(g):
+        x = xs.at[g % 2]
+        for at in range(0, FOLD, 8):
+            rows = (slice(at, at + 8), slice(FOLD + at, FOLD + at + 8))
             for lane in range(0, LANES, 128):
                 lanes = slice(lane, lane + 128)
                 z = [(zs[0, r, lanes], zs[1, r, lanes]) for r in rows]
@@ -309,37 +304,35 @@
                         cre, cim = pairs[p, r, lanes], pairs[p + 1, r, lanes]
                         parts.append((cre * zre - cim * zim, cre * zim + cim * zre))
                     (re1, im1), (re2, im2) = parts
-                    place = wide * j + lane
-                    for put, even, odd in ((place, re1 + re2, im1 - im2), (place + LANES, im1 + im2, re2 - re1)):
-                        for base, value in ((0, even), (FOLD, odd)):
-                            xs[pl.ds(base + at, 16), put : put + 128] = value
-
-        ts[...] = dot_high(w_ref[0], xs[...])
-
-        @pl.loop(0, LPAD // 16)
-        def _(i):
-            at = pl.multiple_of(16 * i, 16)
-            for lane in range(0, GROUP * wide, 256):
-                lanes = slice(lane, lane + 256)
-                hi, lo = split(ts[pl.ds(at, 16), lanes])
-                ss[pl.ds(at, 16), lanes] = hi
-                ss[pl.ds(LPAD + at, 16), lanes] = lo
-                ss[pl.ds(2 * LPAD + at, 16), lanes] = hi
-
-        ys[...] = dot(ah_ref[0], ss[...])
-
-        @pl.loop(0, FOLD // 8)
-        def _(i):
-            at = pl.multiple_of(8 * i, 8)
-            rows = (pl.ds(at, 8), pl.ds(FOLD + at, 8))
+                    put = slice(wide * j + lane, wide * j + lane + 128)
+                    x[rows[0], put] = re1 + re2
+                    x[rows[1], put] = im1 - im2
+                    put = slice(put.start + LANES, put.stop + LANES)
+                    x[rows[0], put] = im1 + im2
+                    x[rows[1], put] = re2 - re1
+
+    def multiply(g):
+        s = ss.at[g % 2]
+        hi, lo = split(dot_high(w_ref[0], xs[g % 2]))
+        s[:LPAD] = hi
+        s[LPAD : 2 * LPAD] = lo
+        s[2 * LPAD : 3 * LPAD] = hi
+        ys[g % 2] = dot(ah_ref[0], s[...])
+
+    def gather(g):
+        for at in range(0, FOLD, 8):
+            rows = (slice(at, at + 8), slice(FOLD + at, FOLD + at + 8))
             for lane in range(0, LANES, 128):
                 lanes = slice(lane, lane + 128)
                 sums = [None] * 4
+                if g > 0:
+                    sums = [acc[r, rows[part], lanes] for part in range(2) for r in range(2)]
                 for j in range(GROUP):
                     p = 2 * (GROUP * g + j)
                     re = slice(wide * j + lane, wide * j + lane + 128)
-                    im = slice(wide * j + LANES + lane, wide * j + LANES + lane + 128)
-                    ure, uim, vre, vim = ys[rows[0], re], ys[rows[0], im], ys[rows[1], re], ys[rows[1], im]
+                    im = slice(re.start + LANES, re.stop + LANES)
+                    ure, uim = ys[g % 2, rows[0], re], ys[g % 2, rows[0], im]
+                    vre, vim = ys[g % 2, rows[1], re], ys[g % 2, rows[1], im]
                     for part, (yre, yim) in enumerate(((ure - vim, uim + vre), (ure + vim, uim - vre))):
                         cre, cim = pairs[p, rows[part], lanes], pairs[p + 1, rows[part], lanes]
                         for r, term in enumerate((cre * yre + cim * yim, cre * yim - cim * yre)):
@@ -347,8 +340,15 @@
                             sums[2 * part + r] = term if old is None else old + term
                 for part in range(2):
                     for r in range(2):
-                        value = sums[2 * part + r]
-                        acc[r, rows[part], lanes] = value + jnp.where(g > 0, acc[r, rows[part], lanes], 0.0)
+                        acc[r, rows[part], lanes] = sums[2 * part + r]
+
+    for g in range(groups + 2):
+        if g < groups:
+            products(g)
+        if 1 <= g <= groups:
+            multiply(g - 1)
+        if g >= 2:
+            gather(g - 2)
 
 
 def clear(*refs):
@@ -359,11 +359,11 @@
 
 
 def first_kernel(pos_ref, base_ref, own_ref, mate_ref, got_ref, gotm_ref, e0, e1, e2, e3, w_ref, ah_ref,
-                 u_ref, pairs, zs, zf, xs, ts, ss, ys, acc):
+                 u_ref, pairs, zs, zf, xs, ss, ys, acc):
     planes = own_ref.shape[0]
     count = e0.shape[2]
     rows = count // HALF
-    clear(pairs, zs, zf, xs, ss, acc)
+    clear(pairs, zs, zf, ss)
 
     @pl.when(pl.program_id(0) == 0)
     def _():
@@ -391,7 +391,7 @@
     for r in range(2):
         zs[r, :, :HALF] = zf[r]
         zs[r, :, HALF : 2 * HALF] = zf[r]
-    normal(pairs, zs, w_ref, ah_ref, xs, ts, ss, ys, acc)
+    normal(pairs, zs, w_ref, ah_ref, xs, ss, ys, acc)
     for r in range(2):
         u_ref[0, r] = zf[r] - 0.5 * (acc[r, :, :HALF] + acc[r, :, HALF : 2 * HALF])
 
@@ -400,10 +400,9 @@
     return [
         pltpu.VMEM((2, ROWS, LANES), F32),
         pltpu.VMEM((2, ROWS, HALF), F32),
-        pltpu.VMEM((ROWS, 2 * GROUP * LANES), F32),
-        pltpu.VMEM((LPAD, 2 * GROUP * LANES), F32),
-        pltpu.VMEM((BACK, 2 * GROUP * LANES), BF),
-        pltpu.VMEM((ROWS, 2 * GROUP * LANES), F32),
+        pltpu.VMEM((2, ROWS, 2 * GROUP * LANES), F32),
+        pltpu.VMEM((2, BACK, 2 * GROUP * LANES), BF),
+        pltpu.VMEM((2, ROWS, 2 * GROUP * LANES), F32),
         pltpu.VMEM((2, ROWS, LANES), F32),
     ]
 
@@ -441,8 +440,8 @@
     )(pos, base, own, mate, got, gotm, *pieces, w, ah)
 
 
-def second_kernel(pos_ref, base_ref, u_ref, keep_ref, got_ref, pairs, w_ref, ah_ref, z_ref, zs, zf, xs, ts, ss, ys, acc):
-    clear(zs, zf, xs, ss, acc)
+def second_kernel(pos_ref, base_ref, u_ref, keep_ref, got_ref, pairs, w_ref, ah_ref, z_ref, zs, zf, xs, ss, ys, acc):
+    clear(zs, zf, ss)
     for k in range(got_ref.shape[1] // (2 * HALF)):
 
         @pl.when(pl.program_id(0) == k)
@@ -458,7 +457,7 @@
         zs[r, :, :HALF] = z
         zs[r, :, HALF : 2 * HALF] = z
         zf[r] = z + zf[r]
-    normal(pairs, zs, w_ref, ah_ref, xs, ts, ss, ys, acc)
+    normal(pairs, zs, w_ref, ah_ref, xs, ss, ys, acc)
     for r in range(2):
         z_ref[0, r] = zf[r] - 0.5 * (acc[r, :, :HALF] + acc[r, :, HALF : 2 * HALF])
 

time: 202 us -> 190 us (0.941)
  Pallas kernels: 113 us -> 96.6 us
  waiting for transfers between devices: 33.3 us -> 37.5 us
    pallas_call x1, Pallas kernels: 38.3 us -> 31.1 us  [first_step(): pl.pallas_call(first_kernel, grid_spec=pltpu.PrefetchScalarGridSpec(num_s...]
    pallas_call x1, Pallas kernels: 27.3 us -> 22.1 us  [second_step(): pl.pallas_call(second_kernel, grid_spec=pltpu.PrefetchScalarGridSpec(num_...]
    ppermute x8, waiting for transfers between devices: 6.62 us -> 10.8 us  [swap(): return lax.ppermute(value, 'coil', [(p, p ^ k) for p in range(4)])]
    pallas_call x1, Pallas kernels: 29.1 us -> 24.9 us  [back_sums(): pl.pallas_call(back_kernel, grid_spec=pltpu.PrefetchScalarGridSpec(num_sc...]
  transfers between devices with their start and end apart: 9 -> 9, of which waited for: 4 -> 5; matrix products, arithmetic and copies ran while one was open for 0% -> 0% of each run, Pallas kernels for 39% -> 36%
where the time goes in v3:
time: 190 us; the launch traced here: 189 us
  Pallas kernels  96.6 us (51%)
  waiting for transfers between devices  37.5 us (20%)
  blocking collectives  30.9 us (16%)
  starting transfers between devices  16.6 us (9%)
  local copies, waits for them, and re-layouts  7.55 us (4%)
    pallas_call x1, Pallas kernels, first_step(): pl.pallas_call(first_kernel, grid_spec=pltpu.PrefetchScalarGridSpec(num_s...  31.1 us
    all_to_all x1, blocking collectives, paired(): lax.all_to_all(result, 'dir', split_axis=0, concat_axis=0, tiled=True)  30.9 us
    all_to_all x1, waiting for transfers between devices, paired(): lax.all_to_all(chunks, ('dir', 'coil'), split_axis=0, concat_axis=0, tile...  26.7 us
    pallas_call x1, Pallas kernels, back_sums(): pl.pallas_call(back_kernel, grid_spec=pltpu.PrefetchScalarGridSpec(num_sc...  24.9 us
    pallas_call x1, Pallas kernels, second_step(): pl.pallas_call(second_kernel, grid_spec=pltpu.PrefetchScalarGridSpec(num_...  22.1 us
    ppermute x8, waiting for transfers between devices, swap(): return lax.ppermute(value, 'coil', [(p, p ^ k) for p in range(4)])  10.8 us
    ppermute x8, starting transfers between devices, swap(): return lax.ppermute(value, 'coil', [(p, p ^ k) for p in range(4)])  8.33 us
    all_to_all x1, starting transfers between devices, paired(): lax.all_to_all(chunks, ('dir', 'coil'), split_axis=0, concat_axis=0, tile...  8.28 us
  transfers between devices with their start and end apart: 9, of which 5 were waited for; matrix products, arithmetic and copies ran while one was open for 0% of the time, Pallas kernels for 36%

profile of v3, /device:TPU:0, one launch (start us, length us, event | category | flops | bytes accessed | tf_op | source)
XLA Modules:
  0.0 189.4 jit_solution(16092081957225833554)
XLA Ops:
  0.0 0.5 collective-permute-start.1
  0.5 2.0 %copy-done.2 = f32[4,2,1,300,300]{4,2,3,1,0:T(1,128)S(1)} copy-done((f32[4,2,1,300,300]{4,2,3,1,0:T(1,128)S(1)}, f32[4,2,1,300,300]{4,2,3,1,0:T(1,128)}, u32[]{:S(2)}) %copy-start.2) | copy-done | bytes 2880024
  2.6 3.7 %folded_maps.1 = (f32[8,320,384]{2,1,0:T(8,128)S(1)}, f32[304,1200]{1,0:T(8,128)}) custom-call(s32[2]{0:T(128)S(1)} %pad_add_fusion.pos_ref, f32[8,300,1,300]{3,2,1,0:T(1,128)S(1)} %bitcast.12), custom_call_target="tpu_custom_call" | custom-call | flops 1000 | bytes 12000 | tf_op jit(solution)/shard_map/folded_maps/pallas_call | solution.py:140
  6.3 1.9 %copy-done = f32[8,320,384]{2,1,0:T(8,128)} copy-done((f32[8,320,384]{2,1,0:T(8,128)}, f32[8,320,384]{2,1,0:T(8,128)S(1)}, u32[]{:S(2)}) %copy-start) | copy-done | bytes 3932184
  8.3 3.0 %collective-permute-start.2 = (f32[304,1200]{1,0:T(8,128)}, f32[304,1200]{1,0:T(8,128)S(1)}, u32[]{:S(2)}, u32[]{:S(2)}) collective-permute-start(f32[304,1200]{1,0:T(8,128)} %get-tuple-element.26), channel_id=1, source_target_pairs={{0,2},{1,3},{2,0},{3,1},{4,6},{5,7},{6,4},{7,5},{8,10},{9,11},{10,... | collective-permute-start | bytes 4377608 | tf_op jit(solution)/shard_map/ppermute | solution.py:599
  11.3 2.4 %estimate_pieces.1 = (f32[3,2,11250]{2,1,0:T(2,128)S(1)}, f32[3,2,11250]{2,1,0:T(2,128)}, f32[3,2,11250]{2,1,0:T(2,128)}, f32[3,2,11250]{2,1,0:T(2,128)}) custom-call(s32[2]{0:T(128)S(1)} %pad_add_fusion.pos_ref, f32[6,2,22500]{2,1,0:T(2,128)S(1)} %copy-done.3), custom_call_target="tpu_custom_call" | custom-call | flops 1000 | bytes 8000 | tf_op jit(solution)/shard_map/estimate_pieces/pallas_call | solution.py:173
  13.7 1.3 collective-permute-done.c1_ref.mate_ref
  15.0 2.6 %collective-permute-start.5 = (f32[3,2,11250]{2,1,0:T(2,128)}, f32[3,2,11250]{2,1,0:T(2,128)}, u32[]{:S(2)}, u32[]{:S(2)}) collective-permute-start(f32[3,2,11250]{2,1,0:T(2,128)} %get-tuple-element.30), channel_id=1, source_target_pairs={{0,3},{1,2},{2,1},{3,0},{4,7},{5,6},{6,5},{7,4},{8,11},{9,10},{10,... | collective-permute-start | bytes 810008 | tf_op jit(solution)/shard_map/ppermute | solution.py:599
  17.8 5.7 %line_matrices.1 = (f32[6,80,320]{2,1,0:T(8,128)S(1)}, bf16[6,320,256]{2,1,0:T(8,128)(2,1)S(1)}) custom-call(s32[6,80,1]{2,1,0:T(8,128)S(1)} %copy.13.lines_ref, f32[300,320]{1,0:T(8,128)S(1)} %copy-done.5, f32[320,300]{1,0:T(8,128)S(1)} %copy-done.4), custom_call_target="tpu_custom_call" | custom-call | flops 1000000 | bytes 1000 | tf_op jit(solution)/shard_map/line_matrices/pallas_call | solution.py:97
  23.6 24.9 %back_sums.1 = (f32[3,2,320,150]{3,2,1,0:T(8,128)S(1)}, f32[304,900]{1,0:T(8,128)S(1)}) custom-call(s32[1]{0:T(128)S(6)} %mul.3.base_ref, s32[2]{0:T(128)S(1)} %pad_add_fusion.pos_ref, f32[6,8,75,1,300]{4,3,2,1,0:T(1,128)} %bitcast.16, f32[6,8,75,1,300]{4,3,2,1,0:T(1,128)} %collective-permute-done.1.k1_ref, f32[8,320,384]{2,1,0:T(8,128)} %copy-done, ...), custom_call_target="tpu_custom_call" | custom-call | flops 14000000 | bytes 22000 | tf_op jit(solution)/shard_map/back_sums/pallas_call | solution.py:266
  48.5 3.7 %collective-permute-done.4.e2 = f32[3,2,11250]{2,1,0:T(2,128)} collective-permute-done((f32[3,2,11250]{2,1,0:T(2,128)}, f32[3,2,11250]{2,1,0:T(2,128)}, u32[]{:S(2)}, u32[]{:S(2)}) %collective-permute-start.4) | collective-permute-done | bytes 270032 | tf_op jit(solution)/shard_map/ppermute | solution.py:599
  52.2 4.5 %collective-permute-done.5.e3 = f32[3,2,11250]{2,1,0:T(2,128)} collective-permute-done((f32[3,2,11250]{2,1,0:T(2,128)}, f32[3,2,11250]{2,1,0:T(2,128)}, u32[]{:S(2)}, u32[]{:S(2)}) %collective-permute-start.5) | collective-permute-done | bytes 270032 | tf_op jit(solution)/shard_map/ppermute | solution.py:599
  56.7 0.5 collective-permute-start.6
  57.2 1.7 collective-permute-start.7
  58.9 1.3 collective-permute-done.6.gotm_ref
  60.2 31.1 %first_step.1 = (f32[3,2,320,150]{3,2,1,0:T(8,128)S(1)}, f32[16,320,384]{2,1,0:T(8,128)}) custom-call(s32[2]{0:T(128)S(1)} %pad_add_fusion.pos_ref, s32[1]{0:T(128)S(6)} %mul.3.base_ref, f32[8,320,384]{2,1,0:T(8,128)} %copy-done, f32[8,320,384]{2,1,0:T(8,128)} %copy-done.7, f32[304,1200]{1,0:T(8,128)S(1)} %collective-permute-done.2.got_ref, ...), custom_call_target="tpu_custom_call" | custom-call | flops 9000000 | bytes 30000 | tf_op jit(solution)/shard_map/first_step/pallas_call | solution.py:421
  91.3 3.2 %copy-done.1 = f32[16,320,384]{2,1,0:T(8,128)S(1)} copy-done((f32[16,320,384]{2,1,0:T(8,128)S(1)}, f32[16,320,384]{2,1,0:T(8,128)}, u32[]{:S(2)}) %copy-start.1) | copy-done | bytes 7864344
  94.6 22.1 %second_step.1.z_ref = f32[3,2,320,150]{3,2,1,0:T(8,128)S(1)} custom-call(s32[2]{0:T(128)S(1)} %pad_add_fusion.pos_ref, s32[1]{0:T(128)S(6)} %mul.3.base_ref, f32[3,2,320,150]{3,2,1,0:T(8,128)S(1)} %get-tuple-element.37.u_ref, f32[3,2,320,150]{3,2,1,0:T(8,128)S(1)} %get-tuple-element.38.keep_ref, f32[304,900]{1,0:T(8,128)S(1)} %collective-permute-done.7.got_ref, ...), custom_call_target="tpu_custom_call" | custom-call | flops 9000000 | bytes 20000 | tf_op jit(solution)/shard_map/second_step/pallas_call | solution.py:468
  116.7 3.2 %flat_chunks.1 = f32[32,3,2,1408]{3,2,1,0:T(2,128)} custom-call(f32[3,2,320,150]{3,2,1,0:T(8,128)S(1)} %second_step.1.z_ref), custom_call_target="tpu_custom_call" | custom-call | flops 1000 | bytes 5000 | tf_op jit(solution)/shard_map/flat_chunks/pallas_call | solution.py:506
  119.9 8.3 %all-to-all-start = ((f32[32,3,2,1408]{3,2,1,0:T(2,128)}), f32[32,3,2,1408]{3,2,1,0:T(2,128)S(1)}, u32[]{:S(2)}, u32[]{:S(2)}) async-start(f32[32,3,2,1408]{3,2,1,0:T(2,128)} %flat_chunks.1), calls=%async_computation | async-start | bytes 2162688 | tf_op jit(solution)/shard_map/all_to_all | solution.py:616
  128.4 26.7 %all-to-all-done.x_ref = f32[32,3,2,1408]{3,2,1,0:T(2,128)S(1)} async-done(((f32[32,3,2,1408]{3,2,1,0:T(2,128)}), f32[32,3,2,1408]{3,2,1,0:T(2,128)S(1)}, u32[]{:S(2)}, u32[]{:S(2)}) %all-to-all-start) | async-done | bytes 1081376 | tf_op jit(solution)/shard_map/all_to_all | solution.py:616
  155.1 1.4 denoise.1
  156.5 30.9 %all_to_all.10.x_ref = f32[8,6,2,2816]{3,2,1,0:T(2,128)S(1)} all-to-all(f32[8,6,2,2816]{3,2,1,0:T(2,128)S(1)} %denoise.1), channel_id=1, replica_groups=mesh['dir'=8,'coil'=4] {'dir'}, dimensions={0} | all-to-all | bytes 2162688 | tf_op jit(solution)/shard_map/all_to_all | solution.py:621
  187.4 2.0 %flat_rows.1 = f32[6,2,22500]{2,1,0:T(2,128)} custom-call(f32[8,6,2,2816]{3,2,1,0:T(2,128)S(1)} %all_to_all.10.x_ref), custom_call_target="tpu_custom_call" | custom-call | flops 1000 | bytes 3000 | tf_op jit(solution)/shard_map/flat_rows/pallas_call | solution.py:573
  (31 shorter events, 0.5 us)
Async XLA Ops:
  0.0 23.6 %collective-permute-start.1 = (f32[6,8,75,1,300]{4,3,2,1,0:T(1,128)}, f32[6,8,75,1,300]{4,3,2,1,0:T(1,128)}, u32[]{:S(2)}, u32[]{:S(2)}) collective-permute-start(f32[6,8,75,1,300]{4,3,2,1,0:T(1,128)} %bitcast.15), channel_id=1, source_target_pairs={{0,1},{1,0},{2,3},{3,2},{4,5},{5,4},{6,7},{7,6},{8,9},{9,8},{10,11... | collective-permute-start | bytes 12960008 | tf_op jit(solution)/shard_map/ppermute | solution.py:599
  0.5 2.0 %copy-start.2 = (f32[4,2,1,300,300]{4,2,3,1,0:T(1,128)S(1)}, f32[4,2,1,300,300]{4,2,3,1,0:T(1,128)}, u32[]{:S(2)}) copy-start(f32[4,2,1,300,300]{4,2,3,1,0:T(1,128)} %param.11) | copy-start | bytes 8640004
  2.6 8.7 %copy-start.3 = (f32[6,2,22500]{2,1,0:T(2,128)S(1)}, f32[6,2,22500]{2,1,0:T(2,128)}, u32[]{:S(2)}) copy-start(f32[6,2,22500]{2,1,0:T(2,128)} %est_ref.1) | copy-start | bytes 3240004
  2.6 15.1 %copy-start.9 = (s32[6,75]{1,0:T(8,128)S(1)}, s32[6,75]{1,0:T(8,128)}, u32[]{:S(2)}) copy-start(s32[6,75]{1,0:T(8,128)} %param.13) | copy-start | bytes 5404
  6.3 1.9 %copy-start = (f32[8,320,384]{2,1,0:T(8,128)}, f32[8,320,384]{2,1,0:T(8,128)S(1)}, u32[]{:S(2)}) copy-start(f32[8,320,384]{2,1,0:T(8,128)S(1)} %get-tuple-element.23.c0_ref.own_ref) | copy-start | bytes 11796484
  6.3 11.5 %copy-start.4 = (f32[320,300]{1,0:T(8,128)S(1)}, f32[320,300]{1,0:T(8,128)}, u32[]{:S(2)}) copy-start(f32[320,300]{1,0:T(8,128)} %constant.39.clone.cols_ref) | copy-start | bytes 1152004
  6.3 11.5 %copy-start.5 = (f32[300,320]{1,0:T(8,128)S(1)}, f32[300,320]{1,0:T(8,128)}, u32[]{:S(2)}) copy-start(f32[300,320]{1,0:T(8,128)} %constant.38.clone.rows_ref) | copy-start | bytes 1152004
  8.2 6.8 %collective-permute-start = (f32[8,320,384]{2,1,0:T(8,128)S(1)}, f32[8,320,384]{2,1,0:T(8,128)S(1)}, u32[]{:S(2)}, u32[]{:S(2)}) collective-permute-start(f32[8,320,384]{2,1,0:T(8,128)S(1)} %get-tuple-element.23.c0_ref.own_ref), channel_id=1, source_target_pairs={{0,1},{1,0},{2,3},{3,2},{4,5},{5,4},{6,7},{7,6},{8,9},{9,8},{10,11... | collective-permute-start | bytes 11796488 | tf_op jit(solution)/shard_map/ppermute | solution.py:599
  8.3 48.4 %collective-permute-start.2 = (f32[304,1200]{1,0:T(8,128)}, f32[304,1200]{1,0:T(8,128)S(1)}, u32[]{:S(2)}, u32[]{:S(2)}) collective-permute-start(f32[304,1200]{1,0:T(8,128)} %get-tuple-element.26), channel_id=1, source_target_pairs={{0,2},{1,3},{2,0},{3,1},{4,6},{5,7},{6,4},{7,5},{8,10},{9,11},{10,... | collective-permute-start | bytes 4377608 | tf_op jit(solution)/shard_map/ppermute | solution.py:599
  13.7 34.8 %collective-permute-start.3 = (f32[3,2,11250]{2,1,0:T(2,128)}, f32[3,2,11250]{2,1,0:T(2,128)S(1)}, u32[]{:S(2)}, u32[]{:S(2)}) collective-permute-start(f32[3,2,11250]{2,1,0:T(2,128)} %get-tuple-element.28), channel_id=1, source_target_pairs={{0,1},{1,0},{2,3},{3,2},{4,5},{5,4},{6,7},{7,6},{8,9},{9,8},{10,11... | collective-permute-start | bytes 810008 | tf_op jit(solution)/shard_map/ppermute | solution.py:599
  13.7 38.5 %collective-permute-start.4 = (f32[3,2,11250]{2,1,0:T(2,128)}, f32[3,2,11250]{2,1,0:T(2,128)}, u32[]{:S(2)}, u32[]{:S(2)}) collective-permute-start(f32[3,2,11250]{2,1,0:T(2,128)} %get-tuple-element.29), channel_id=1, source_target_pairs={{0,2},{1,3},{2,0},{3,1},{4,6},{5,7},{6,4},{7,5},{8,10},{9,11},{10,... | collective-permute-start | bytes 810008 | tf_op jit(solution)/shard_map/ppermute | solution.py:599
  15.0 2.6 %copy-start.7 = (f32[8,320,384]{2,1,0:T(8,128)}, f32[8,320,384]{2,1,0:T(8,128)S(1)}, u32[]{:S(2)}) copy-start(f32[8,320,384]{2,1,0:T(8,128)S(1)} %collective-permute-done.c1_ref.mate_ref) | copy-start | bytes 11796484
  15.0 41.7 %collective-permute-start.5 = (f32[3,2,11250]{2,1,0:T(2,128)}, f32[3,2,11250]{2,1,0:T(2,128)}, u32[]{:S(2)}, u32[]{:S(2)}) collective-permute-start(f32[3,2,11250]{2,1,0:T(2,128)} %get-tuple-element.30), channel_id=1, source_target_pairs={{0,3},{1,2},{2,1},{3,0},{4,7},{5,6},{6,5},{7,4},{8,11},{9,10},{10,... | collective-permute-start | bytes 810008 | tf_op jit(solution)/shard_map/ppermute | solution.py:599
  56.7 3.5 %collective-permute-start.6 = (f32[304,1200]{1,0:T(8,128)S(1)}, f32[304,1200]{1,0:T(8,128)S(1)}, u32[]{:S(2)}, u32[]{:S(2)}) collective-permute-start(f32[304,1200]{1,0:T(8,128)S(1)} %collective-permute-done.2.got_ref), channel_id=1, source_target_pairs={{0,1},{1,0},{2,3},{3,2},{4,5},{5,4},{6,7},{7,6},{8,9},{9,8},{10,11... | collective-permute-start | bytes 4377608 | tf_op jit(solution)/shard_map/ppermute | solution.py:599
  57.2 34.1 %collective-permute-start.7 = (f32[304,900]{1,0:T(8,128)S(1)}, f32[304,900]{1,0:T(8,128)S(1)}, u32[]{:S(2)}, u32[]{:S(2)}) collective-permute-start(f32[304,900]{1,0:T(8,128)S(1)} %get-tuple-element.39), channel_id=1, source_target_pairs={{0,2},{1,3},{2,0},{3,1},{4,6},{5,7},{6,4},{7,5},{8,10},{9,11},{10,... | collective-permute-start | bytes 3283208 | tf_op jit(solution)/shard_map/ppermute | solution.py:599
  91.3 3.2 %copy-start.1 = (f32[16,320,384]{2,1,0:T(8,128)S(1)}, f32[16,320,384]{2,1,0:T(8,128)}, u32[]{:S(2)}) copy-start(f32[16,320,384]{2,1,0:T(8,128)} %get-tuple-element.40.pairs) | copy-start | bytes 23592964
  119.9 8.3 %copy-start.8 = (f32[48,2,96]{2,1,0:T(2,128)S(1)}, f32[48,2,96]{2,1,0:T(2,128)}, u32[]{:S(2)}) copy-start(f32[48,2,96]{2,1,0:T(2,128)} %param.14) | copy-start | bytes 110596
  119.9 8.4 %copy-start.10 = (f32[96]{0:T(128)S(1)}, f32[96]{0:T(128)}, u32[]{:S(2)}) copy-start(f32[96]{0:T(128)} %param.15) | copy-start | bytes 1156
  119.9 35.2 %copy-start.6 = (f32[96,48,2]{0,2,1:T(2,128)S(1)}, f32[96,48,2]{0,2,1:T(2,128)}, u32[]{:S(2)}) copy-start(f32[96,48,2]{0,2,1:T(2,128)} %param.16) | copy-start | bytes 110596
  119.9 35.2 %all-to-all-start = ((f32[32,3,2,1408]{3,2,1,0:T(2,128)}), f32[32,3,2,1408]{3,2,1,0:T(2,128)S(1)}, u32[]{:S(2)}, u32[]{:S(2)}) async-start(f32[32,3,2,1408]{3,2,1,0:T(2,128)} %flat_chunks.1), calls=%async_computation | async-start | bytes 2162688 | tf_op jit(solution)/shard_map/all_to_all | solution.py:616
